TPU v7x, 128 devices: a whole 4x4x4 slice. The times are simulated.
128 devices in a mesh: row: 16 (over x_lo, y, core), col: 8 (over x_hi, z).
Axes of the slice: x: 4 (x_hi: 2, x_lo: 2; x = x_hi * 2 + x_lo), y: 4, z: 4, core: 2. Of those that a mesh axis runs over, the one named last changes fastest.
Arguments:
- features: bfloat16 [16384, 1408], P(('row', 'col')), may hold values from -8 to 8
- proj_weight: bfloat16 [1408, 1024], replicated, may hold values from -1.5 to 1.5
- image_vals: bfloat16 [16384, 1024], P(('row', 'col')), may hold values from -1 to 1
- image_scales: bfloat16 [16384, 8], P(('row', 'col')), may hold values from 0.05 to 1
- text_vals: bfloat16 [16384, 1024], P(('row', 'col')), may hold values from -1 to 1
- text_scales: bfloat16 [16384, 8], P(('row', 'col')), may hold values from 0.05 to 1
- logit_scale: float32 [1], replicated, may hold values from 30 to 180
Outputs:
- loss: float32 [], replicated
- grad_w: float32 [1408, 1024], replicated
All inputs are finite; a program needn't handle non-finite values.
Results may differ from a plain program's by a relative error of at most 0.0003.
The roundings to bfloat16 on the way count: a program that leaves them out, or rounds other values in their place, can miss the bound.
Values may be sent and summed in bfloat16 or wider, within the bound.
No kernel may reach another device: no remote copies, remote signals or barrier semaphores. Data moves between devices by JAX's collectives and lax.ppermute only.
A program may use at most 128 MiB of HBM per device.

v0:
```python
import functools
import jax
import jax.numpy as jnp
from jax import lax
from jax.experimental import pallas as pl
from jax.experimental.pallas import tpu as pltpu
from jax.sharding import PartitionSpec as P

EPS = 1e-06
LOG2E = 1.4426950408889634
LN2 = 0.6931471805599453
SAFE = 60.0
AXES = ("row", "col")
X_POINT = (1, 0, 3, 2)
X_TARGET = (3, 2, 1, 0)
LANES = 128
WIDE = 2 * LANES
BATCHES = (((0, 0), (1, 0), (0, 1), (0, 3)), ((1, 3), (0, 2), (1, 1)), ((1, 2),))
ORDER = [(core,) + place for batch in BATCHES for core in range(2) for place in batch]
POINT_ORDER = tuple(range(8))


def device_index(x, y, z, core):
    row = ((x % 2) * 4 + y % 4) * 2 + core
    col = (x // 2) * 4 + z % 4
    return row * 8 + col


def take_from(value, x_map=None, dy=0, dz=0, flip=0):
    perm = []
    for x in range(4):
        source_x = x if x_map is None else x_map[x]
        for y in range(4):
            for z in range(4):
                for core in range(2):
                    source = device_index(source_x, y + dy, z + dz, core ^ flip)
                    perm.append((source, device_index(x, y, z, core)))
    return lax.ppermute(value, AXES, perm)


def whole():
    return pl.BlockSpec(memory_space=pltpu.VMEM)


def scalars():
    return pl.BlockSpec(memory_space=pltpu.SMEM)


def anywhere():
    return pl.BlockSpec(memory_space=pl.ANY)


def params(mib, grid=False):
    return pltpu.CompilerParams(
        vmem_limit_bytes=mib * 2**20, **({"dimension_semantics": ("arbitrary",)} if grid else {})
    )


def canonical(block):
    core, flip, step = block
    return (core * 2 + flip) * 4 + step


def unit_kernel(image_ref, image_scale_ref, text_ref, text_scale_ref, out_ref):
    count, width = image_ref.shape
    blocks = image_scale_ref.shape[0]
    size = width // blocks
    for which, (vals, scales_ref) in enumerate(
        ((image_ref, image_scale_ref), (text_ref, text_scale_ref))
    ):
        scales = scales_ref[...].astype(jnp.float32)
        scales = jnp.concatenate([scales] * (count // blocks), axis=0).T
        full = [
            vals[:, k * size : (k + 1) * size].astype(jnp.float32) * scales[:, k : k + 1]
            for k in range(blocks)
        ]
        square = sum(jnp.sum(part * part, axis=-1, keepdims=True) for part in full)
        inv = lax.rsqrt(square + EPS)
        for k in range(blocks):
            out_ref[which * count : (which + 1) * count, k * size : (k + 1) * size] = (
                full[k] * inv
            ).astype(jnp.bfloat16)


def unit_targets(image_vals, image_scales, text_vals, text_scales):
    count, width = image_vals.shape
    return pl.pallas_call(
        unit_kernel,
        out_shape=jax.ShapeDtypeStruct((2 * count, width), jnp.bfloat16),
        in_specs=[whole()] * 4,
        out_specs=whole(),
        compiler_params=params(58),
        cost_estimate=pl.CostEstimate(flops=2**20, bytes_accessed=2**20, transcendentals=0),
    )(image_vals, image_scales.T, text_vals, text_scales.T)


def proj_kernel(*refs):
    feature_refs = refs[:8]
    weight_ref, tile_ref, proj_ref, unit_ref = refs[8:]
    step = pl.program_id(0)
    rows = feature_refs[0].shape[0]
    for turn in range(2):

        @pl.when(step == turn)
        def _():
            for k in range(4):
                tile_ref[k * rows : (k + 1) * rows, :] = feature_refs[4 * turn + k][...]

    proj = jnp.dot(tile_ref[...], weight_ref[...], preferred_element_type=jnp.float32)
    inv = lax.rsqrt(jnp.sum(proj * proj, axis=-1, keepdims=True) + EPS)
    proj_ref[...] = proj
    unit_ref[...] = (proj * inv).astype(jnp.bfloat16)


def project(features, weight):
    deep, width = weight.shape
    step = 4 * features[0].shape[0]
    once = pl.Buffered(1)

    def rows_of(array_width):
        return pl.BlockSpec((step, array_width), lambda i: (i, 0))

    return pl.pallas_call(
        proj_kernel,
        grid=(2,),
        out_shape=(
            jax.ShapeDtypeStruct((2 * step, deep), jnp.bfloat16),
            jax.ShapeDtypeStruct((2 * step, width), jnp.float32),
            jax.ShapeDtypeStruct((2 * step, width), jnp.bfloat16),
        ),
        in_specs=[pl.BlockSpec(part.shape, lambda i: (0, 0), pipeline_mode=once) for part in features]
        + [pl.BlockSpec((deep, width), lambda i: (0, 0), pipeline_mode=once)],
        out_specs=(rows_of(deep), rows_of(width), rows_of(width)),
        compiler_params=params(58, True),
        cost_estimate=pl.CostEstimate(
            flops=4 * step * deep * width, bytes_accessed=12 * 2**20, transcendentals=0
        ),
    )(*features, weight)


def to_column(row):
    parts = []
    for at in range(0, row.shape[1], LANES):
        wide = jnp.broadcast_to(row[:, at : at + LANES], (LANES, LANES))
        parts.append(wide.T)
    return jnp.concatenate(parts, axis=0)


def logits_kernel(count, first, last, *refs):
    refs = list(refs)
    scale_ref, points_ref = refs[:2]
    target_refs = refs[2 : 2 + count]
    refs = refs[2 + count :]
    if not first:
        old_max_ref, old_sum_ref = refs[:2]
        refs = refs[2:]
    if last:
        old_col_refs = refs[:2]
        refs = refs[2:]
    logits_ref, col_ref = refs[:2]
    refs = refs[2:]
    if first:
        diag_ref = refs.pop(0)
    if last:
        row_ref, all_col_ref = refs[:2]
        refs = refs[2:]
    row_max_ref, row_sum_ref, held_ref, col_max_ref, sem_ref = refs
    rows = points_ref.shape[0]
    chunk = 64
    scale = scale_ref[0] * LOG2E

    def copy_out(j):
        at = slice(j * WIDE, (j + 1) * WIDE)
        return pltpu.make_async_copy(held_ref.at[:, at], logits_ref.at[:, at], sem_ref.at[j])

    for j in range(count):
        at = slice(j * WIDE, (j + 1) * WIDE)
        held_ref[:, at] = scale * lax.dot_general(
            points_ref[...],
            target_refs[j][...],
            (((1,), (1,)), ((), ())),
            preferred_element_type=jnp.float32,
        )
        copy_out(j).start()
        top = None
        for r in range(0, rows, chunk):
            value = held_ref[r : r + chunk, at]
            if j:
                row_max_ref[r : r + chunk, :] = jnp.maximum(row_max_ref[r : r + chunk, :], value)
            elif first:
                row_max_ref[r : r + chunk, :] = value
            else:
                row_max_ref[r : r + chunk, :] = jnp.maximum(old_max_ref[r : r + chunk, :], value)
            part = jnp.max(value.reshape(chunk // 8, 8, WIDE), axis=0)
            top = part if top is None else jnp.maximum(top, part)
        col_max_ref[j : j + 1, :] = jnp.max(top, axis=0, keepdims=True)

    if first:
        rows_at = lax.broadcasted_iota(jnp.int32, (LANES, WIDE), 0)
        cols_at = lax.broadcasted_iota(jnp.int32, (LANES, WIDE), 1) % LANES
        own = jnp.where(rows_at == cols_at, held_ref[:LANES, :WIDE], 0.0)
        diag_ref[...] = jnp.broadcast_to(jnp.sum(own, axis=0, keepdims=True), diag_ref.shape)
        row_sum_ref[...] = jnp.zeros(row_sum_ref.shape, jnp.float32)
    else:
        row_sum_ref[...] = old_sum_ref[...] * jnp.exp2(old_max_ref[...] - row_max_ref[...])

    def sums(j, _):
        at = pl.ds(pl.multiple_of(j * WIDE, WIDE), WIDE)
        top = col_max_ref[pl.ds(j, 1), :]
        total = jnp.zeros((8, WIDE), jnp.float32)
        for r in range(0, rows, chunk):
            value = held_ref[r : r + chunk, at]
            row_sum_ref[r : r + chunk, :] += jnp.exp2(value - row_max_ref[r : r + chunk, :])
            total += jnp.sum(jnp.exp2(value - top).reshape(chunk // 8, 8, WIDE), axis=0)
        col_ref[pl.ds(j, 1), :] = top + jnp.log(jnp.sum(total, axis=0, keepdims=True)) * LOG2E
        return 0

    lax.fori_loop(0, count, sums, 0)
    if last:
        k = 0
        for source in (*old_col_refs, col_ref):
            for at in range(source.shape[0]):
                to = canonical(ORDER[k])
                all_col_ref[to : to + 1, :] = source[at : at + 1, :]
                k += 1
        for which in range(2):
            lanes = slice(which * LANES, (which + 1) * LANES)
            for r in range(0, rows, LANES):
                tops = row_max_ref[r : r + LANES, lanes].T
                part = row_sum_ref[r : r + LANES, lanes].T
                top = jnp.max(tops, axis=0, keepdims=True)
                total = jnp.sum(part * jnp.exp2(tops - top), axis=0, keepdims=True)
                row_ref[which : which + 1, r : r + LANES] = top + jnp.log(total) * LOG2E
    for j in range(count):
        copy_out(j).wait()


def logits_of(points, scale, targets, old, old_cols):
    rows = points.shape[0]
    count = len(targets)
    cols = count * WIDE
    first, last = not old, bool(old_cols)
    lanes = jax.ShapeDtypeStruct((rows, WIDE), jnp.float32)
    held = [pltpu.VMEM(lanes.shape, jnp.float32)] * 2
    outs = [
        jax.ShapeDtypeStruct((rows, cols), jnp.float32),
        jax.ShapeDtypeStruct((count, WIDE), jnp.float32),
    ]
    if first:
        outs.append(jax.ShapeDtypeStruct((8, WIDE), jnp.float32))
    if last:
        outs.append(jax.ShapeDtypeStruct((2, rows), jnp.float32))
        outs.append(jax.ShapeDtypeStruct((16, WIDE), jnp.float32))
    else:
        outs += [lanes, lanes]
    return pl.pallas_call(
        functools.partial(logits_kernel, count, first, last),
        out_shape=outs,
        in_specs=[scalars()] + [whole()] * (1 + count + len(old) + len(old_cols)),
        out_specs=[pl.BlockSpec(memory_space=pl.ANY)] + [whole()] * (len(outs) - 1),
        scratch_shapes=(held if last else [])
        + [
            pltpu.VMEM((rows, cols), jnp.float32),
            pltpu.VMEM((count, WIDE), jnp.float32),
            pltpu.SemaphoreType.DMA((count,)),
        ],
        compiler_params=params(58),
        cost_estimate=pl.CostEstimate(
            flops=2 * rows * cols * points.shape[1],
            bytes_accessed=4 * rows * cols,
            transcendentals=2 * rows * cols,
        ),
    )(scale, points, *targets, *old, *old_cols)


def grad_kernel(place_ref, scale_ref, *refs):
    logits_refs = refs[:3]
    target_refs = refs[3:19]
    row_ref, all_col_ref, diag_ref, proj_ref, turned_any, kept_ref, sent_ref, loss_ref = refs[19:27]
    coef_ref, targets_ref, tops_ref, shares_ref, edges_ref, high_ref, low_ref = refs[27:34]
    part_ref, turned_ref, sem_ref = refs[34:]
    step = pl.program_id(0)
    size = proj_ref.shape[0]
    scale = scale_ref[0]
    chunk = 64

    def copy_in(k):
        if k == 16:
            return pltpu.make_async_copy(turned_any, turned_ref, sem_ref.at[k])
        return pltpu.make_async_copy(
            target_refs[k], targets_ref.at[k * WIDE : (k + 1) * WIDE, :], sem_ref.at[k]
        )

    peak = jnp.max(row_ref[...])
    near = peak - jnp.min(all_col_ref[...]) < SAFE

    @pl.when(step == 0)
    def _():
        for k in range(17):
            copy_in(k).start()
        for k, block in enumerate(ORDER):
            at = canonical(block)
            edges_ref[k : k + 1, :] = all_col_ref[at : at + 1, :]
        for k, place in enumerate(POINT_ORDER):
            for which in range(2):
                row = row_ref[which : which + 1, place * LANES : (place + 1) * LANES]
                r_at = slice(k * LANES, (k + 1) * LANES)
                lanes = slice(which * LANES, (which + 1) * LANES)
                tops_ref[r_at, lanes] = to_column(row)
                shares_ref[r_at, lanes] = to_column(jnp.exp2(row - peak))
        both = edges_ref[:1, :] - 2.0 * diag_ref[:1, :]
        both = both[:, :LANES] + both[:, LANES:] + row_ref[:1, :LANES] + row_ref[1:2, :LANES]
        loss_ref[...] = jnp.broadcast_to(both, loss_ref.shape)

    def own_hits(r):
        rows_at = lax.broadcasted_iota(jnp.int32, (chunk, WIDE), 0) + r + step * size
        cols_at = lax.broadcasted_iota(jnp.int32, (chunk, WIDE), 1) % LANES
        return jnp.where(rows_at == cols_at, 2.0, 0.0)

    def coefs(is_near):
        k = 0
        for logits_ref in logits_refs:
            for at in range(0, logits_ref.shape[1], WIDE):
                edge = edges_ref[k : k + 1, :]
                rise = jnp.exp2(peak - edge)
                for r in range(0, size, chunk):
                    value = logits_ref[r : r + chunk, at : at + WIDE]
                    r_at = pl.ds(pl.multiple_of(step * size + r, chunk), chunk)
                    coef = jnp.exp2(value - tops_ref[r_at, :])
                    if is_near:
                        coef = coef + coef * (shares_ref[r_at, :] * rise)
                    else:
                        coef = coef + jnp.exp2(value - edge)
                    if k == 0 and r < LANES:
                        coef = coef - own_hits(r)
                    coef_ref[r : r + chunk, k * WIDE : (k + 1) * WIDE] = coef.astype(jnp.bfloat16)
                k += 1

    @pl.when(near)
    def _():
        coefs(True)

    @pl.when(jnp.logical_not(near))
    def _():
        coefs(False)

    @pl.when(step == 0)
    def _():
        for k in range(16):
            copy_in(k).wait()

    grad = jnp.dot(coef_ref[...], targets_ref[...], preferred_element_type=jnp.float32)
    grad = grad * (scale * 0.25)
    proj = proj_ref[...]
    inv = lax.rsqrt(jnp.sum(proj * proj, axis=-1, keepdims=True) + EPS)
    along = jnp.sum(proj * grad, axis=-1, keepdims=True)
    grad = inv * (grad - along * inv * inv * proj)
    high = grad.astype(jnp.bfloat16)
    rows = pl.ds(pl.multiple_of(step * size, size), size)
    high_ref[rows, :] = high
    low_ref[rows, :] = (grad - high.astype(jnp.float32)).astype(jnp.bfloat16)

    @pl.when(step == pl.num_programs(0) - 1)
    def _():
        copy_in(16).wait()
        core = place_ref[0]
        deep = turned_ref.shape[0]
        cut = deep // 16

        def products(n, _):
            at = pl.ds(pl.multiple_of(n * WIDE, WIDE), WIDE)
            part_ref[...] = jnp.dot(
                turned_ref[...], high_ref[:, at], preferred_element_type=jnp.float32
            ) + jnp.dot(turned_ref[...], low_ref[:, at], preferred_element_type=jnp.float32)
            for v in range(8):
                for side in range(2):
                    lanes = slice(side * LANES, (side + 1) * LANES)
                    for out_ref, half in ((kept_ref, core), (sent_ref, 1 - core)):
                        from_row = pl.multiple_of(half * (deep // 2) + v * cut, 8)
                        out_ref[v * 8 + 2 * n + side] = part_ref[pl.ds(from_row, cut), lanes]
            return 0

        lax.fori_loop(0, high_ref.shape[1] // WIDE, products, 0)


def grad_of(place, scale, logits, targets, row_lse, col_lse, diag, proj, turned):
    rows, width = proj.shape
    deep = turned.shape[0]
    step = 256
    cut = deep // 16
    piece = jax.ShapeDtypeStruct((64, cut, LANES), jnp.float32)
    cols = sum(part.shape[1] for part in logits)
    return pl.pallas_call(
        grad_kernel,
        grid=(rows // step,),
        out_shape=(piece, piece, jax.ShapeDtypeStruct((8, LANES), jnp.float32)),
        in_specs=[scalars(), scalars()]
        + [pl.BlockSpec((step, part.shape[1]), lambda i: (i, 0)) for part in logits]
        + [anywhere()] * len(targets)
        + [whole(), whole(), whole()]
        + [pl.BlockSpec((step, width), lambda i: (i, 0)), anywhere()],
        out_specs=(whole(), whole(), whole()),
        scratch_shapes=[
            pltpu.VMEM((step, cols), jnp.bfloat16),
            pltpu.VMEM((cols, width), jnp.bfloat16),
            pltpu.VMEM((rows, WIDE), jnp.float32),
            pltpu.VMEM((rows, WIDE), jnp.float32),
            pltpu.VMEM((16, WIDE), jnp.float32),
            pltpu.VMEM((rows, width), jnp.bfloat16),
            pltpu.VMEM((rows, width), jnp.bfloat16),
            pltpu.VMEM((deep, WIDE), jnp.float32),
            pltpu.VMEM((deep, rows), jnp.bfloat16),
            pltpu.SemaphoreType.DMA((len(targets) + 1,)),
        ],
        compiler_params=params(58, True),
        cost_estimate=pl.CostEstimate(
            flops=2 * rows * cols * width, bytes_accessed=32 * 2**20, transcendentals=rows * cols
        ),
    )(place, scale, *logits, *targets, row_lse, col_lse, diag, proj, turned)


def assemble_kernel(place_ref, here_ref, there_ref, out_ref, loss_ref, held_ref, sem_ref):
    cut = here_ref.shape[1] - 8
    half = 8 * cut
    copies = []
    loss = jnp.zeros((1, LANES), jnp.float32)
    for turn, ref in enumerate((here_ref, there_ref)):
        from_row = pl.multiple_of((place_ref[0] ^ turn) * half, 8)
        for v in range(8):
            for w in range(8):
                flags = [ref[v * 8 + w, cut + k : cut + k + 1, :] for k in range(4)]
                held_ref[turn, v * cut : (v + 1) * cut, w * LANES : (w + 1) * LANES] = ref[
                    v * 8 + w, :cut
                ] * jnp.exp2(-flags[0])
                loss += flags[1] * 16.0 + flags[2] / 64.0 + flags[3] / 16384.0
        copy = pltpu.make_async_copy(
            held_ref.at[turn], out_ref.at[pl.ds(from_row, half), :], sem_ref.at[turn]
        )
        copy.start()
        copies.append(copy)
    loss_ref[...] = jnp.broadcast_to(loss, loss_ref.shape)
    for copy in copies:
        copy.wait()


def assemble(place, here, there):
    cut = here.shape[1] - 8
    return pl.pallas_call(
        assemble_kernel,
        in_specs=[scalars(), whole(), whole()],
        out_specs=(anywhere(), whole()),
        out_shape=(
            jax.ShapeDtypeStruct((16 * cut, 8 * LANES), jnp.float32),
            jax.ShapeDtypeStruct((8, LANES), jnp.float32),
        ),
        scratch_shapes=[
            pltpu.VMEM((2, 8 * cut, 8 * LANES), jnp.float32),
            pltpu.SemaphoreType.DMA((2,)),
        ],
        compiler_params=params(16),
        cost_estimate=pl.CostEstimate(flops=2**20, bytes_accessed=9 * 2**20, transcendentals=0),
    )(place, here, there)


def same_core_group(x, y, z, core):
    return (core,), (x, y, z)


def groups_of(rule):
    found = {}
    for x in range(4):
        for y in range(4):
            for z in range(4):
                for core in range(2):
                    group, place = rule(x, y, z, core)
                    found.setdefault(group, []).append((place, device_index(x, y, z, core)))
    return [[device for _, device in sorted(found[group])] for group in sorted(found)]


def swap_blocks(value, rule):
    return lax.all_to_all(
        value, AXES, split_axis=0, concat_axis=0, axis_index_groups=groups_of(rule), tiled=True
    )


def merged(value, got):
    low, high = jnp.minimum(value, got), jnp.maximum(value, got)
    return high + jnp.log(1.0 + jnp.exp2(low - high)) * LOG2E


def exchange_statistics(rows, cols):
    row_shape = (2, 2, 4, rows.shape[1] // 8)
    col_shape = (2, 2, 4, cols.shape[1])

    def row_add(value, got):
        return merged(value, got.reshape(rows.shape))

    def col_add(value, got):
        return merged(value, got.reshape(cols.shape))

    got_rows = take_from(rows, x_map=X_POINT)
    got_cols = take_from(cols, flip=1)
    rows = row_add(rows, got_rows.reshape(row_shape)[:, ::-1])
    cols = col_add(cols, got_cols.reshape(col_shape)[::-1])
    rows, cols = lax.optimization_barrier((rows, cols))
    got_rows = take_from(rows, dz=1)
    got_cols = take_from(cols, x_map=X_TARGET)
    rows = row_add(rows, jnp.roll(got_rows.reshape(row_shape), 1, axis=2))
    cols = col_add(cols, got_cols.reshape(col_shape)[:, ::-1])
    rows, cols = lax.optimization_barrier((rows, cols))
    got_rows = take_from(rows, dz=2)
    got_cols = take_from(cols, dy=1)
    rows = row_add(rows, jnp.roll(got_rows.reshape(row_shape), 2, axis=2))
    cols = col_add(cols, jnp.roll(got_cols.reshape(col_shape), 1, axis=2))
    got_cols = take_from(cols, dy=2)
    return rows, col_add(cols, jnp.roll(got_cols.reshape(col_shape), 2, axis=2))


def gather_points(own):
    def near(value):
        return take_from(value, x_map=X_POINT)

    beside, after, before = near(own), take_from(own, dz=1), take_from(own, dz=-1)
    beside_before, far, beside_after = take_from(beside, dz=-1), take_from(after, dz=1), near(after)
    beside_far = take_from(beside_after, dz=1)
    return [own, after, far, before, beside, beside_after, beside_far, beside_before]


def gather_targets(own):
    def near(value):
        return take_from(value, x_map=X_TARGET)

    def with_other(blocks):
        return blocks + [take_from(block, flip=1) for block in blocks]

    beside, after, before = near(own), take_from(own, dy=1), take_from(own, dy=-1)
    first = with_other([own, beside, after, before])
    beside_before, far, beside_after = take_from(beside, dy=-1), take_from(after, dy=1), near(after)
    second = with_other([beside_before, far, beside_after])
    third = with_other([take_from(beside_after, dy=1)])
    return [first, second, third]


def total_sum(place, kept, sent, local_loss):
    count, cut, lanes = kept.shape
    half = kept + take_from(sent, flip=1)
    own = jnp.sum(swap_blocks(half, same_core_group), axis=0)
    power = 14.0 - jnp.floor(jnp.log2(jnp.maximum(jnp.max(jnp.abs(own)), 1e-30)))
    small = (own * jnp.exp2(power)).astype(jnp.float16)
    first = (local_loss / 16.0).astype(jnp.float16)
    rest = local_loss - first.astype(jnp.float32) * 16.0
    second = (rest * 64.0).astype(jnp.float16)
    rest = rest - second.astype(jnp.float32) / 64.0
    third = (rest * 16384.0).astype(jnp.float16)
    values = [power.astype(jnp.float16), first, second, third]
    tail = jnp.stack([values[min(i, 3)] for i in range(8)])
    tail = jnp.broadcast_to(tail[:, None], (8, lanes))
    small = jnp.concatenate([small, tail], axis=0)
    here = swap_blocks(jnp.broadcast_to(small, (count,) + small.shape), same_core_group)
    there = take_from(here, flip=1)
    grad_w, loss = assemble(place, here.astype(jnp.float32), there.astype(jnp.float32))
    return grad_w, loss[0, 0]


def body(features, proj_weight, image_vals, image_scales, text_vals, text_scales, logit_scale):
    rows = features.shape[0]
    total = rows * lax.axis_size("row") * lax.axis_size("col")
    place = (lax.axis_index("row") % 2).astype(jnp.int32).reshape(1)

    own = unit_targets(image_vals, image_scales, text_vals, text_scales)
    targets = gather_targets(own)
    tile, proj, points = project(gather_points(features), proj_weight)
    turned = tile.T
    first, near_cols, diag, *old = logits_of(points, logit_scale, targets[0], (), ())
    second, far_cols, *old = logits_of(points, logit_scale, targets[1], old, ())
    third, _, rows_part, cols_part = logits_of(
        points, logit_scale, targets[2], old, (near_cols, far_cols)
    )
    row_lse, col_lse = exchange_statistics(rows_part, cols_part)
    kept, sent, losses = grad_of(
        place,
        logit_scale,
        (first, second, third),
        sum(targets, []),
        row_lse,
        col_lse,
        diag,
        proj,
        turned,
    )
    grad_w, loss = total_sum(place, kept, sent, jnp.sum(losses[0]) * LN2)
    return (loss / (4.0 * total), grad_w)


def solution(mesh):
    return jax.shard_map(
        body,
        mesh=mesh,
        in_specs=(
            P(("row", "col"), None),
            P(),
            P(("row", "col"), None),
            P(("row", "col"), None),
            P(("row", "col"), None),
            P(("row", "col"), None),
            P(),
        ),
        out_specs=(P(), P()),
        check_vma=False,
    )
```

profile of v0, /device:TPU:1, one launch (start us, length us, event | category | flops | bytes accessed | tf_op | source)
XLA Modules:
  0.0 245.1 jit_solution(10461552163847013594)
XLA Ops:
  0.6 2.5 %collective-permute-start.2 = (bf16[128,1408]{1,0:T(8,128)(2,1)}, bf16[128,1408]{1,0:T(8,128)(2,1)S(1)}, u32[]{:S(2)}, u32[]{:S(2)}) collective-permute-start(bf16[128,1408]{1,0:T(8,128)(2,1)} %refs_0_.4), channel_id=1, source_target_pairs={{3,0},{11,8},{0,1},{8,9},{1,2},{9,10},{2,3},{10,11},{19,16},{27,24... | collective-permute-start | bytes 1081352 | tf_op jit(solution)/shard_map/ppermute | solution.py:38
  3.2 2.2 collective-permute-start
  5.4 1.2 collective-permute-start.3
  6.6 2.5 %shard_map.87.refs_2_.refs_3_ = bf16[256,1024]{1,0:T(8,128)(2,1)} custom-call(bf16[128,1024]{1,0:T(8,128)(2,1)} %image_ref.1, bf16[8,128]{1,0:T(8,128)(2,1)} %bitcast.14, bf16[128,1024]{1,0:T(8,128)(2,1)} %text_ref.1, bf16[8,128]{1,0:T(8,128)(2,1)} %bitcast.15), custom_call_target="tpu_custom_call" | custom-call | flops 1048576 | bytes 1048576 | tf_op jit(solution)/shard_map/pallas_call | solution.py:87
  9.1 1.2 collective-permute-start.10
  10.4 1.3 collective-permute-start.9
  11.7 2.0 collective-permute-done.2.refs_3_
  13.6 2.7 %collective-permute-start.8 = (bf16[256,1024]{1,0:T(8,128)(2,1)}, bf16[256,1024]{1,0:T(8,128)(2,1)S(1)}, u32[]{:S(2)}, u32[]{:S(2)}) collective-permute-start(bf16[256,1024]{1,0:T(8,128)(2,1)} %shard_map.87.refs_2_.refs_3_), channel_id=1, source_target_pairs={{16,0},{24,8},{17,1},{25,9},{18,2},{26,10},{19,3},{27,11},{32,16},... | collective-permute-start | bytes 1572872 | tf_op jit(solution)/shard_map/ppermute | solution.py:38
  16.4 2.5 %collective-permute-start.7 = (bf16[256,1024]{1,0:T(8,128)(2,1)}, bf16[256,1024]{1,0:T(8,128)(2,1)S(1)}, u32[]{:S(2)}, u32[]{:S(2)}) collective-permute-start(bf16[256,1024]{1,0:T(8,128)(2,1)} %shard_map.87.refs_2_.refs_3_), channel_id=1, source_target_pairs={{68,0},{76,8},{69,1},{77,9},{70,2},{78,10},{71,3},{79,11},{84,16},... | collective-permute-start | bytes 1572872 | tf_op jit(solution)/shard_map/ppermute | solution.py:38
  18.9 1.2 collective-permute-start.1
  20.1 5.4 %collective-permute-done.9.refs_5_.refs_6_ = bf16[256,1024]{1,0:T(8,128)(2,1)S(1)} collective-permute-done((bf16[256,1024]{1,0:T(8,128)(2,1)}, bf16[256,1024]{1,0:T(8,128)(2,1)S(1)}, u32[]{:S(2)}, u32[]{:S(2)}) %collective-permute-start.9) | collective-permute-done | bytes 524320 | tf_op jit(solution)/shard_map/ppermute | solution.py:38
  25.5 1.2 collective-permute-done.8.refs_4_.refs_5_
  26.7 2.1 collective-permute-start.13
  28.8 0.9 collective-permute-done.7.refs_3_.refs_4_
  29.7 2.5 %collective-permute-start.16 = (bf16[256,1024]{1,0:T(8,128)(2,1)S(1)}, bf16[256,1024]{1,0:T(8,128)(2,1)S(1)}, u32[]{:S(2)}, u32[]{:S(2)}) collective-permute-start(bf16[256,1024]{1,0:T(8,128)(2,1)S(1)} %collective-permute-done.8.refs_4_.refs_5_), channel_id=1, source_target_pairs={{68,0},{76,8},{69,1},{77,9},{70,2},{78,10},{71,3},{79,11},{84,16},... | collective-permute-start | bytes 1572872 | tf_op jit(solution)/shard_map/ppermute | solution.py:38
  32.2 2.4 collective-permute-start.15
  34.6 1.1 collective-permute-start.12
  35.7 0.2 collective-permute-done.6.refs_7_
  35.9 0.9 collective-permute-start.14
  36.8 1.1 collective-permute-start.5
  38.0 4.0 %collective-permute-done.16.refs_4_.refs_13_ = bf16[256,1024]{1,0:T(8,128)(2,1)S(1)} collective-permute-done((bf16[256,1024]{1,0:T(8,128)(2,1)S(1)}, bf16[256,1024]{1,0:T(8,128)(2,1)S(1)}, u32[]{:S(2)}, u32[]{:S(2)}) %collective-permute-start.16) | collective-permute-done | bytes 524320 | tf_op jit(solution)/shard_map/ppermute | solution.py:38
  41.9 4.5 %collective-permute-start.20 = (bf16[256,1024]{1,0:T(8,128)(2,1)S(1)}, bf16[256,1024]{1,0:T(8,128)(2,1)S(1)}, u32[]{:S(2)}, u32[]{:S(2)}) collective-permute-start(bf16[256,1024]{1,0:T(8,128)(2,1)S(1)} %collective-permute-done.16.refs_4_.refs_13_), channel_id=1, source_target_pairs={{16,0},{24,8},{17,1},{25,9},{18,2},{26,10},{19,3},{27,11},{32,16},... | collective-permute-start | bytes 1572872 | tf_op jit(solution)/shard_map/ppermute | solution.py:38
  46.4 1.7 collective-permute-start.11
  49.0 2.5 %collective-permute-start.18 = (bf16[256,1024]{1,0:T(8,128)(2,1)S(1)}, bf16[256,1024]{1,0:T(8,128)(2,1)}, u32[]{:S(2)}, u32[]{:S(2)}) collective-permute-start(bf16[256,1024]{1,0:T(8,128)(2,1)S(1)} %collective-permute-done.15.refs_3_.refs_12_), channel_id=1, source_target_pairs={{8,0},{0,8},{9,1},{1,9},{10,2},{2,10},{11,3},{3,11},{24,16},{16,24... | collective-permute-start | bytes 1572872 | tf_op jit(solution)/shard_map/ppermute | solution.py:38
  51.5 0.7 copy-done.18
  52.3 8.6 %shard_map.86 = (bf16[1024,1408]{1,0:T(8,128)(2,1)}, f32[1024,1024]{1,0:T(8,128)}, bf16[1024,1024]{1,0:T(8,128)(2,1)}) custom-call(bf16[128,1408]{1,0:T(8,128)(2,1)} %refs_0_.4, bf16[128,1408]{1,0:T(8,128)(2,1)} %copy-done.13, bf16[128,1408]{1,0:T(8,128)(2,1)} %copy-done.16, bf16[128,1408]{1,0:T(8,128)(2,1)} %copy-done.12, bf16[128,1408]{1,0:T(8,128)(2,1)} %copy-done.14, ...), custom_call_target="tpu_custom_call" | custom-call | flops 2952790016 | bytes 12582912 | tf_op jit(solution)/shard_map/pallas_call | solution.py:123
  61.0 0.7 collective-permute-start.21
  61.7 12.0 %shard_map.88 = (f32[1024,2048]{1,0:T(8,128)}, f32[8,256]{1,0:T(8,128)}, f32[8,256]{1,0:T(8,128)}, f32[1024,256]{1,0:T(8,128)}, f32[1024,256]{1,0:T(8,128)}) custom-call(f32[1]{0:T(128)S(6)} %copy.10.refs_0_.scale_ref, bf16[1024,1024]{1,0:T(8,128)(2,1)} %get-tuple-element.26.refs_1_, bf16[256,1024]{1,0:T(8,128)(2,1)} %shard_map.87.refs_2_.refs_3_, ...), custom_call_target="tpu_custom_call" | custom-call | flops 4294967296 | bytes 8388608 | tf_op jit(solution)/shard_map/pallas_call | solution.py:256
  73.8 10.6 %shard_map.89 = (f32[1024,1536]{1,0:T(8,128)}, f32[6,256]{1,0:T(8,128)}, f32[1024,256]{1,0:T(8,128)}, f32[1024,256]{1,0:T(8,128)}) custom-call(f32[1]{0:T(128)S(6)} %copy.10.refs_0_.scale_ref, bf16[1024,1024]{1,0:T(8,128)(2,1)} %get-tuple-element.26.refs_1_, bf16[256,1024]{1,0:T(8,128)(2,1)} %copy-done.11, bf16[256,1024]{1,0:T(8,128)(2,1)} %copy-done.9, ...), custom_call_target="tpu_custom_call" | custom-call | flops 3221225472 | bytes 6291456 | tf_op jit(solution)/shard_map/pallas_call | solution.py:256
  84.4 0.8 copy-done.2
  85.2 6.2 %shard_map.90 = (f32[1024,512]{1,0:T(8,128)}, f32[2,256]{1,0:T(2,128)}, f32[2,1024]{1,0:T(2,128)}, f32[16,256]{1,0:T(8,128)}) custom-call(f32[1]{0:T(128)S(6)} %copy.10.refs_0_.scale_ref, bf16[1024,1024]{1,0:T(8,128)(2,1)} %get-tuple-element.26.refs_1_, bf16[256,1024]{1,0:T(8,128)(2,1)} %copy-done.1, bf16[256,1024]{1,0:T(8,128)(2,1)} %copy-done.2, ...), custom_call_target="tpu_custom_call" | custom-call | flops 1073741824 | bytes 2097152 | tf_op jit(solution)/shard_map/pallas_call | solution.py:256
  91.4 0.4 collective-permute-start.22
  91.7 0.3 collective-permute-start.23
  92.1 2.1 collective-permute-done.22
  94.2 0.7 multiply_add_fusion.6
  95.0 0.7 multiply_add_fusion.3
  95.7 1.9 collective-permute-start.24
  97.7 0.4 collective-permute-start.25
  98.1 0.4 collective-permute-done.24
  98.5 2.9 %collective-permute-done.25 = f32[16,256]{1,0:T(8,128)S(1)} collective-permute-done((f32[16,256]{1,0:T(8,128)S(1)}, f32[16,256]{1,0:T(8,128)S(1)}, u32[]{:S(2)}, u32[]{:S(2)}) %collective-permute-start.25) | collective-permute-done | bytes 16416 | tf_op jit(solution)/shard_map/ppermute | solution.py:38
  101.5 0.3 collective-permute-start.26
  101.9 2.9 %copy.9 = bf16[1024,1408]{0,1:T(8,128)(2,1)} copy(bf16[1024,1408]{1,0:T(8,128)(2,1)S(1)} %copy-done) | data formatting | bytes 5767168 | tf_op jit(solution)/shard_map/pallas_call | solution.py:123
  104.7 1.1 collective-permute-done.26
  105.9 1.4 collective-permute-done.27
  107.5 0.6 multiply_add_fusion.4.refs_19_
  108.1 3.5 %collective-permute-done.28 = f32[16,256]{1,0:T(8,128)S(1)} collective-permute-done((f32[16,256]{1,0:T(8,128)S(1)}, f32[16,256]{1,0:T(8,128)S(1)}, u32[]{:S(2)}, u32[]{:S(2)}) %collective-permute-start.28) | collective-permute-done | bytes 16416 | tf_op jit(solution)/shard_map/ppermute | solution.py:38
  111.6 0.6 multiply_add_fusion.refs_20_
  112.3 30.5 %shard_map.91 = (f32[64,88,128]{2,1,0:T(8,128)}, f32[64,88,128]{2,1,0:T(8,128)}, f32[8,128]{1,0:T(8,128)}) custom-call(s32[1]{0:T(128)} %bitcast.place_ref, f32[1]{0:T(128)S(6)} %copy.10.refs_0_.scale_ref, f32[1024,2048]{1,0:T(8,128)} %get-tuple-element.27.refs_0_, f32[1024,1536]{1,0:T(8,128)} %get-tuple-element.30.refs_1_, ...), custom_call_target="tpu_custom_call" | custom-call | flops 8589934592 | bytes 33554432 | tf_op jit(solution)/shard_map/pallas_call | solution.py:393
  142.8 5.0 %collective-permute-start.29 = (f32[64,88,128]{2,1,0:T(8,128)}, f32[64,88,128]{2,1,0:T(8,128)S(1)}, u32[]{:S(2)}, u32[]{:S(2)}) collective-permute-start(f32[64,88,128]{2,1,0:T(8,128)} %get-tuple-element.46), channel_id=1, source_target_pairs={{8,0},{0,8},{9,1},{1,9},{10,2},{2,10},{11,3},{3,11},{24,16},{16,24... | collective-permute-start | bytes 8650760 | tf_op jit(solution)/shard_map/ppermute | solution.py:38
  147.8 5.1 %collective-permute-done.29 = f32[64,88,128]{2,1,0:T(8,128)S(1)} collective-permute-done((f32[64,88,128]{2,1,0:T(8,128)}, f32[64,88,128]{2,1,0:T(8,128)S(1)}, u32[]{:S(2)}, u32[]{:S(2)}) %collective-permute-start.29) | collective-permute-done | bytes 2883616 | tf_op jit(solution)/shard_map/ppermute | solution.py:38
  152.9 3.7 %add.64 = f32[64,88,128]{2,1,0:T(8,128)} add(f32[64,88,128]{2,1,0:T(8,128)} %get-tuple-element.45, f32[64,88,128]{2,1,0:T(8,128)S(1)} %collective-permute-done.29) | non-fusion elementwise | flops 720896 | bytes 8650752 | tf_op jit(solution)/shard_map/add | solution.py:546
  156.6 8.0 %all-to-all-start = ((f32[64,88,128]{2,1,0:T(8,128)}), f32[64,88,128]{2,1,0:T(8,128)S(1)}, u32[]{:S(2)}, u32[]{:S(2)}) async-start(f32[64,88,128]{2,1,0:T(8,128)} %add.64), calls=%async_computation | async-start | bytes 5767168 | tf_op jit(solution)/shard_map/all_to_all | solution.py:481
  164.6 1.3 slice_reduce_fusion
  167.2 34.0 %all-to-all-done = f32[64,88,128]{2,1,0:T(8,128)S(1)} async-done(((f32[64,88,128]{2,1,0:T(8,128)}), f32[64,88,128]{2,1,0:T(8,128)S(1)}, u32[]{:S(2)}, u32[]{:S(2)}) %all-to-all-start) | async-done | bytes 2883616 | tf_op jit(solution)/shard_map/all_to_all | solution.py:481
  201.2 0.2 reduce_sum.18
  201.3 0.6 abs_reduce_fusion
  203.0 0.2 broadcast_in_dim.10
  203.2 29.7 %all_to_all.10 = f16[64,96,128]{2,1,0:T(8,128)(2,1)S(1)} all-to-all(f16[64,96,128]{2,1,0:T(8,128)(2,1)S(1)} %broadcast_in_dim.10), channel_id=1, replica_groups={{0,1,2,3,16,17,18,19,32,33,34,35,48,49,50,51,64,65,66,67,80,81,82,83,96..., dimensions={0} | all-to-all | bytes 3145728 | tf_op jit(solution)/shard_map/all_to_all | solution.py:481
  232.9 3.6 %collective-permute-start.30 = (f16[64,96,128]{2,1,0:T(8,128)(2,1)S(1)}, f16[64,96,128]{2,1,0:T(8,128)(2,1)S(1)}, u32[]{:S(2)}, u32[]{:S(2)}) collective-permute-start(f16[64,96,128]{2,1,0:T(8,128)(2,1)S(1)} %all_to_all.10), channel_id=1, source_target_pairs={{8,0},{0,8},{9,1},{1,9},{10,2},{2,10},{11,3},{3,11},{24,16},{16,24... | collective-permute-start | bytes 4718600 | tf_op jit(solution)/shard_map/ppermute | solution.py:38
  236.5 0.4 convert_element_type.34.here_ref
  236.9 2.6 %collective-permute-done.30 = f16[64,96,128]{2,1,0:T(8,128)(2,1)S(1)} collective-permute-done((f16[64,96,128]{2,1,0:T(8,128)(2,1)S(1)}, f16[64,96,128]{2,1,0:T(8,128)(2,1)S(1)}, u32[]{:S(2)}, u32[]{:S(2)}) %collective-permute-start.30) | collective-permute-done | bytes 1572896 | tf_op jit(solution)/shard_map/ppermute | solution.py:38
  239.5 0.4 convert_element_type.35.there_ref
  239.9 2.8 %shard_map.92 = (f32[1408,1024]{1,0:T(8,128)}, f32[8,128]{1,0:T(8,128)S(1)}) custom-call(s32[1]{0:T(128)} %bitcast.place_ref, f32[64,96,128]{2,1,0:T(8,128)S(1)} %convert_element_type.34.here_ref, f32[64,96,128]{2,1,0:T(8,128)S(1)} %convert_element_type.35.there_ref), custom_call_target="tpu_custom_call" | custom-call | flops 1048576 | bytes 9437184 | tf_op jit(solution)/shard_map/pallas_call | solution.py:448
  242.8 0.5 slice.47
  (91 shorter events, 1.1 us)
Async XLA Ops:
  0.6 13.0 %collective-permute-start.2 = (bf16[128,1408]{1,0:T(8,128)(2,1)}, bf16[128,1408]{1,0:T(8,128)(2,1)S(1)}, u32[]{:S(2)}, u32[]{:S(2)}) collective-permute-start(bf16[128,1408]{1,0:T(8,128)(2,1)} %refs_0_.4), channel_id=1, source_target_pairs={{3,0},{11,8},{0,1},{8,9},{1,2},{9,10},{2,3},{10,11},{19,16},{27,24... | collective-permute-start | bytes 1081352 | tf_op jit(solution)/shard_map/ppermute | solution.py:38
  3.2 13.2 %collective-permute-start = (bf16[128,1408]{1,0:T(8,128)(2,1)}, bf16[128,1408]{1,0:T(8,128)(2,1)S(1)}, u32[]{:S(2)}, u32[]{:S(2)}) collective-permute-start(bf16[128,1408]{1,0:T(8,128)(2,1)} %refs_0_.4), channel_id=1, source_target_pairs={{1,0},{9,8},{2,1},{10,9},{3,2},{11,10},{0,3},{8,11},{17,16},{25,24... | collective-permute-start | bytes 1081352 | tf_op jit(solution)/shard_map/ppermute | solution.py:38
  5.4 13.5 %collective-permute-start.3 = (bf16[128,1408]{1,0:T(8,128)(2,1)}, bf16[128,1408]{1,0:T(8,128)(2,1)S(1)}, u32[]{:S(2)}, u32[]{:S(2)}) collective-permute-start(bf16[128,1408]{1,0:T(8,128)(2,1)} %refs_0_.4), channel_id=1, source_target_pairs={{64,0},{72,8},{65,1},{73,9},{66,2},{74,10},{67,3},{75,11},{80,16},... | collective-permute-start | bytes 1081352 | tf_op jit(solution)/shard_map/ppermute | solution.py:38
  9.1 9.8 %collective-permute-start.10 = (bf16[256,1024]{1,0:T(8,128)(2,1)}, bf16[256,1024]{1,0:T(8,128)(2,1)S(1)}, u32[]{:S(2)}, u32[]{:S(2)}) collective-permute-start(bf16[256,1024]{1,0:T(8,128)(2,1)} %shard_map.87.refs_2_.refs_3_), channel_id=1, source_target_pairs={{8,0},{0,8},{9,1},{1,9},{10,2},{2,10},{11,3},{3,11},{24,16},{16,24... | collective-permute-start | bytes 1572872 | tf_op jit(solution)/shard_map/ppermute | solution.py:38
  10.4 15.1 %collective-permute-start.9 = (bf16[256,1024]{1,0:T(8,128)(2,1)}, bf16[256,1024]{1,0:T(8,128)(2,1)S(1)}, u32[]{:S(2)}, u32[]{:S(2)}) collective-permute-start(bf16[256,1024]{1,0:T(8,128)(2,1)} %shard_map.87.refs_2_.refs_3_), channel_id=1, source_target_pairs={{48,0},{56,8},{49,1},{57,9},{50,2},{58,10},{51,3},{59,11},{0,16},{... | collective-permute-start | bytes 1572872 | tf_op jit(solution)/shard_map/ppermute | solution.py:38
  13.6 38.6 %copy-start.12 = (bf16[128,1408]{1,0:T(8,128)(2,1)}, bf16[128,1408]{1,0:T(8,128)(2,1)S(1)}, u32[]{:S(2)}) copy-start(bf16[128,1408]{1,0:T(8,128)(2,1)S(1)} %collective-permute-done.2.refs_3_) | copy-start | bytes 1081348
  13.6 13.0 %collective-permute-start.8 = (bf16[256,1024]{1,0:T(8,128)(2,1)}, bf16[256,1024]{1,0:T(8,128)(2,1)S(1)}, u32[]{:S(2)}, u32[]{:S(2)}) collective-permute-start(bf16[256,1024]{1,0:T(8,128)(2,1)} %shard_map.87.refs_2_.refs_3_), channel_id=1, source_target_pairs={{16,0},{24,8},{17,1},{25,9},{18,2},{26,10},{19,3},{27,11},{32,16},... | collective-permute-start | bytes 1572872 | tf_op jit(solution)/shard_map/ppermute | solution.py:38
  16.4 18.3 %copy-start.13 = (bf16[128,1408]{1,0:T(8,128)(2,1)}, bf16[128,1408]{1,0:T(8,128)(2,1)S(1)}, u32[]{:S(2)}) copy-start(bf16[128,1408]{1,0:T(8,128)(2,1)S(1)} %collective-permute-done.refs_1_) | copy-start | bytes 1081348
  16.4 13.3 %collective-permute-start.7 = (bf16[256,1024]{1,0:T(8,128)(2,1)}, bf16[256,1024]{1,0:T(8,128)(2,1)S(1)}, u32[]{:S(2)}, u32[]{:S(2)}) collective-permute-start(bf16[256,1024]{1,0:T(8,128)(2,1)} %shard_map.87.refs_2_.refs_3_), channel_id=1, source_target_pairs={{68,0},{76,8},{69,1},{77,9},{70,2},{78,10},{71,3},{79,11},{84,16},... | collective-permute-start | bytes 1572872 | tf_op jit(solution)/shard_map/ppermute | solution.py:38
  18.9 16.9 %copy-start.14 = (bf16[128,1408]{1,0:T(8,128)(2,1)}, bf16[128,1408]{1,0:T(8,128)(2,1)S(1)}, u32[]{:S(2)}) copy-start(bf16[128,1408]{1,0:T(8,128)(2,1)S(1)} %collective-permute-done.3.refs_4_) | copy-start | bytes 1081348
  18.9 13.3 %collective-permute-start.4 = (bf16[128,1408]{1,0:T(8,128)(2,1)S(1)}, bf16[128,1408]{1,0:T(8,128)(2,1)S(1)}, u32[]{:S(2)}, u32[]{:S(2)}) collective-permute-start(bf16[128,1408]{1,0:T(8,128)(2,1)S(1)} %collective-permute-done.refs_1_), channel_id=1, source_target_pairs={{64,0},{72,8},{65,1},{73,9},{66,2},{74,10},{67,3},{75,11},{80,16},... | collective-permute-start | bytes 1081352 | tf_op jit(solution)/shard_map/ppermute | solution.py:38
  18.9 42.0 %copy-start.3 = (bf16[256,1024]{1,0:T(8,128)(2,1)}, bf16[256,1024]{1,0:T(8,128)(2,1)S(1)}, u32[]{:S(2)}) copy-start(bf16[256,1024]{1,0:T(8,128)(2,1)S(1)} %collective-permute-done.10.refs_6_.refs_7_) | copy-start | bytes 1572868
  18.9 15.7 %collective-permute-start.1 = (bf16[128,1408]{1,0:T(8,128)(2,1)S(1)}, bf16[128,1408]{1,0:T(8,128)(2,1)S(1)}, u32[]{:S(2)}, u32[]{:S(2)}) collective-permute-start(bf16[128,1408]{1,0:T(8,128)(2,1)S(1)} %collective-permute-done.refs_1_), channel_id=1, source_target_pairs={{1,0},{9,8},{2,1},{10,9},{3,2},{11,10},{0,3},{8,11},{17,16},{25,24... | collective-permute-start | bytes 1081352 | tf_op jit(solution)/shard_map/ppermute | solution.py:38
  25.5 35.5 %copy-start.4 = (bf16[256,1024]{1,0:T(8,128)(2,1)}, bf16[256,1024]{1,0:T(8,128)(2,1)S(1)}, u32[]{:S(2)}) copy-start(bf16[256,1024]{1,0:T(8,128)(2,1)S(1)} %collective-permute-done.9.refs_5_.refs_6_) | copy-start | bytes 1572868
  25.5 10.4 %collective-permute-start.6 = (bf16[128,1408]{1,0:T(8,128)(2,1)S(1)}, bf16[128,1408]{1,0:T(8,128)(2,1)S(1)}, u32[]{:S(2)}, u32[]{:S(2)}) collective-permute-start(bf16[128,1408]{1,0:T(8,128)(2,1)S(1)} %collective-permute-done.3.refs_4_), channel_id=1, source_target_pairs={{3,0},{11,8},{0,1},{8,9},{1,2},{9,10},{2,3},{10,11},{19,16},{27,24... | collective-permute-start | bytes 1081352 | tf_op jit(solution)/shard_map/ppermute | solution.py:38
  26.7 34.3 %copy-start.5 = (bf16[256,1024]{1,0:T(8,128)(2,1)}, bf16[256,1024]{1,0:T(8,128)(2,1)S(1)}, u32[]{:S(2)}) copy-start(bf16[256,1024]{1,0:T(8,128)(2,1)S(1)} %collective-permute-done.8.refs_4_.refs_5_) | copy-start | bytes 1572868
  26.7 10.1 %collective-permute-start.13 = (bf16[256,1024]{1,0:T(8,128)(2,1)S(1)}, bf16[256,1024]{1,0:T(8,128)(2,1)S(1)}, u32[]{:S(2)}, u32[]{:S(2)}) collective-permute-start(bf16[256,1024]{1,0:T(8,128)(2,1)S(1)} %collective-permute-done.9.refs_5_.refs_6_), channel_id=1, source_target_pairs={{8,0},{0,8},{9,1},{1,9},{10,2},{2,10},{11,3},{3,11},{24,16},{16,24... | collective-permute-start | bytes 1572872 | tf_op jit(solution)/shard_map/ppermute | solution.py:38
  29.7 31.2 %copy-start.6 = (bf16[256,1024]{1,0:T(8,128)(2,1)}, bf16[256,1024]{1,0:T(8,128)(2,1)S(1)}, u32[]{:S(2)}) copy-start(bf16[256,1024]{1,0:T(8,128)(2,1)S(1)} %collective-permute-done.7.refs_3_.refs_4_) | copy-start | bytes 1572868
  29.7 12.2 %collective-permute-start.16 = (bf16[256,1024]{1,0:T(8,128)(2,1)S(1)}, bf16[256,1024]{1,0:T(8,128)(2,1)S(1)}, u32[]{:S(2)}, u32[]{:S(2)}) collective-permute-start(bf16[256,1024]{1,0:T(8,128)(2,1)S(1)} %collective-permute-done.8.refs_4_.refs_5_), channel_id=1, source_target_pairs={{68,0},{76,8},{69,1},{77,9},{70,2},{78,10},{71,3},{79,11},{84,16},... | collective-permute-start | bytes 1572872 | tf_op jit(solution)/shard_map/ppermute | solution.py:38
  32.2 19.3 %copy-start.15 = (bf16[128,1408]{1,0:T(8,128)(2,1)}, bf16[128,1408]{1,0:T(8,128)(2,1)S(1)}, u32[]{:S(2)}) copy-start(bf16[128,1408]{1,0:T(8,128)(2,1)S(1)} %collective-permute-done.4.refs_5_) | copy-start | bytes 1081348
  32.2 14.2 %collective-permute-start.15 = (bf16[256,1024]{1,0:T(8,128)(2,1)S(1)}, bf16[256,1024]{1,0:T(8,128)(2,1)S(1)}, u32[]{:S(2)}, u32[]{:S(2)}) collective-permute-start(bf16[256,1024]{1,0:T(8,128)(2,1)S(1)} %collective-permute-done.8.refs_4_.refs_5_), channel_id=1, source_target_pairs={{16,0},{24,8},{17,1},{25,9},{18,2},{26,10},{19,3},{27,11},{32,16},... | collective-permute-start | bytes 1572872 | tf_op jit(solution)/shard_map/ppermute | solution.py:38
  34.6 11.8 %copy-start.16 = (bf16[128,1408]{1,0:T(8,128)(2,1)}, bf16[128,1408]{1,0:T(8,128)(2,1)S(1)}, u32[]{:S(2)}) copy-start(bf16[128,1408]{1,0:T(8,128)(2,1)S(1)} %collective-permute-done.1.refs_2_) | copy-start | bytes 1081348
  34.6 14.1 %collective-permute-start.12 = (bf16[256,1024]{1,0:T(8,128)(2,1)S(1)}, bf16[256,1024]{1,0:T(8,128)(2,1)S(1)}, u32[]{:S(2)}, u32[]{:S(2)}) collective-permute-start(bf16[256,1024]{1,0:T(8,128)(2,1)S(1)} %collective-permute-done.8.refs_4_.refs_5_), channel_id=1, source_target_pairs={{8,0},{0,8},{9,1},{1,9},{10,2},{2,10},{11,3},{3,11},{24,16},{16,24... | collective-permute-start | bytes 1572872 | tf_op jit(solution)/shard_map/ppermute | solution.py:38
  35.9 10.5 %copy-start.17 = (bf16[128,1408]{1,0:T(8,128)(2,1)}, bf16[128,1408]{1,0:T(8,128)(2,1)S(1)}, u32[]{:S(2)}) copy-start(bf16[128,1408]{1,0:T(8,128)(2,1)S(1)} %collective-permute-done.6.refs_7_) | copy-start | bytes 1081348
  35.9 13.0 %collective-permute-start.14 = (bf16[256,1024]{1,0:T(8,128)(2,1)S(1)}, bf16[256,1024]{1,0:T(8,128)(2,1)S(1)}, u32[]{:S(2)}, u32[]{:S(2)}) collective-permute-start(bf16[256,1024]{1,0:T(8,128)(2,1)S(1)} %collective-permute-done.7.refs_3_.refs_4_), channel_id=1, source_target_pairs={{48,0},{56,8},{49,1},{57,9},{50,2},{58,10},{51,3},{59,11},{0,16},{... | collective-permute-start | bytes 1572872 | tf_op jit(solution)/shard_map/ppermute | solution.py:38
  36.8 24.1 %copy-start.7 = (bf16[256,1024]{1,0:T(8,128)(2,1)}, bf16[256,1024]{1,0:T(8,128)(2,1)S(1)}, u32[]{:S(2)}) copy-start(bf16[256,1024]{1,0:T(8,128)(2,1)S(1)} %collective-permute-done.13.refs_9_.refs_10_) | copy-start | bytes 1572868
  36.8 14.7 %collective-permute-start.5 = (bf16[128,1408]{1,0:T(8,128)(2,1)S(1)}, bf16[128,1408]{1,0:T(8,128)(2,1)S(1)}, u32[]{:S(2)}, u32[]{:S(2)}) collective-permute-start(bf16[128,1408]{1,0:T(8,128)(2,1)S(1)} %collective-permute-done.4.refs_5_), channel_id=1, source_target_pairs={{1,0},{9,8},{2,1},{10,9},{3,2},{11,10},{0,3},{8,11},{17,16},{25,24... | collective-permute-start | bytes 1081352 | tf_op jit(solution)/shard_map/ppermute | solution.py:38
  41.9 19.1 %copy-start.8 = (bf16[256,1024]{1,0:T(8,128)(2,1)}, bf16[256,1024]{1,0:T(8,128)(2,1)S(1)}, u32[]{:S(2)}) copy-start(bf16[256,1024]{1,0:T(8,128)(2,1)S(1)} %collective-permute-done.16.refs_4_.refs_13_) | copy-start | bytes 1572868
  41.9 19.1 %collective-permute-start.20 = (bf16[256,1024]{1,0:T(8,128)(2,1)S(1)}, bf16[256,1024]{1,0:T(8,128)(2,1)S(1)}, u32[]{:S(2)}, u32[]{:S(2)}) collective-permute-start(bf16[256,1024]{1,0:T(8,128)(2,1)S(1)} %collective-permute-done.16.refs_4_.refs_13_), channel_id=1, source_target_pairs={{16,0},{24,8},{17,1},{25,9},{18,2},{26,10},{19,3},{27,11},{32,16},... | collective-permute-start | bytes 1572872 | tf_op jit(solution)/shard_map/ppermute | solution.py:38
  46.4 14.6 %copy-start.9 = (bf16[256,1024]{1,0:T(8,128)(2,1)}, bf16[256,1024]{1,0:T(8,128)(2,1)S(1)}, u32[]{:S(2)}) copy-start(bf16[256,1024]{1,0:T(8,128)(2,1)S(1)} %collective-permute-done.15.refs_3_.refs_12_) | copy-start | bytes 1572868
  46.4 15.3 %collective-permute-start.11 = (bf16[256,1024]{1,0:T(8,128)(2,1)S(1)}, bf16[256,1024]{1,0:T(8,128)(2,1)}, u32[]{:S(2)}, u32[]{:S(2)}) collective-permute-start(bf16[256,1024]{1,0:T(8,128)(2,1)S(1)} %collective-permute-done.7.refs_3_.refs_4_), channel_id=1, source_target_pairs={{8,0},{0,8},{9,1},{1,9},{10,2},{2,10},{11,3},{3,11},{24,16},{16,24... | collective-permute-start | bytes 1572872 | tf_op jit(solution)/shard_map/ppermute | solution.py:38
  48.7 12.2 %copy-start.10 = (bf16[256,1024]{1,0:T(8,128)(2,1)}, bf16[256,1024]{1,0:T(8,128)(2,1)S(1)}, u32[]{:S(2)}) copy-start(bf16[256,1024]{1,0:T(8,128)(2,1)S(1)} %collective-permute-done.12.refs_8_.refs_9_) | copy-start | bytes 1572868
  48.8 25.0 %collective-permute-start.19 = (bf16[256,1024]{1,0:T(8,128)(2,1)S(1)}, bf16[256,1024]{1,0:T(8,128)(2,1)}, u32[]{:S(2)}, u32[]{:S(2)}) collective-permute-start(bf16[256,1024]{1,0:T(8,128)(2,1)S(1)} %collective-permute-done.16.refs_4_.refs_13_), channel_id=1, source_target_pairs={{8,0},{0,8},{9,1},{1,9},{10,2},{2,10},{11,3},{3,11},{24,16},{16,24... | collective-permute-start | bytes 1572872 | tf_op jit(solution)/shard_map/ppermute | solution.py:38
  49.0 12.0 %copy-start.11 = (bf16[256,1024]{1,0:T(8,128)(2,1)}, bf16[256,1024]{1,0:T(8,128)(2,1)S(1)}, u32[]{:S(2)}) copy-start(bf16[256,1024]{1,0:T(8,128)(2,1)S(1)} %collective-permute-done.14.refs_2_.refs_11_) | copy-start | bytes 1572868
  49.0 24.8 %collective-permute-start.18 = (bf16[256,1024]{1,0:T(8,128)(2,1)S(1)}, bf16[256,1024]{1,0:T(8,128)(2,1)}, u32[]{:S(2)}, u32[]{:S(2)}) collective-permute-start(bf16[256,1024]{1,0:T(8,128)(2,1)S(1)} %collective-permute-done.15.refs_3_.refs_12_), channel_id=1, source_target_pairs={{8,0},{0,8},{9,1},{1,9},{10,2},{2,10},{11,3},{3,11},{24,16},{16,24... | collective-permute-start | bytes 1572872 | tf_op jit(solution)/shard_map/ppermute | solution.py:38
  51.5 0.7 copy-start.18
  52.2 21.5 %collective-permute-start.17 = (bf16[256,1024]{1,0:T(8,128)(2,1)S(1)}, bf16[256,1024]{1,0:T(8,128)(2,1)}, u32[]{:S(2)}, u32[]{:S(2)}) collective-permute-start(bf16[256,1024]{1,0:T(8,128)(2,1)S(1)} %collective-permute-done.14.refs_2_.refs_11_), channel_id=1, source_target_pairs={{8,0},{0,8},{9,1},{1,9},{10,2},{2,10},{11,3},{3,11},{24,16},{16,24... | collective-permute-start | bytes 1572872 | tf_op jit(solution)/shard_map/ppermute | solution.py:38
  61.0 12.7 %copy-start.1 = (bf16[256,1024]{1,0:T(8,128)(2,1)}, bf16[256,1024]{1,0:T(8,128)(2,1)S(1)}, u32[]{:S(2)}) copy-start(bf16[256,1024]{1,0:T(8,128)(2,1)S(1)} %collective-permute-done.20.refs_2_.refs_17_) | copy-start | bytes 1572868
  61.0 23.3 %collective-permute-start.21 = (bf16[256,1024]{1,0:T(8,128)(2,1)S(1)}, bf16[256,1024]{1,0:T(8,128)(2,1)S(1)}, u32[]{:S(2)}, u32[]{:S(2)}) collective-permute-start(bf16[256,1024]{1,0:T(8,128)(2,1)S(1)} %collective-permute-done.20.refs_2_.refs_17_), channel_id=1, source_target_pairs={{8,0},{0,8},{9,1},{1,9},{10,2},{2,10},{11,3},{3,11},{24,16},{16,24... | collective-permute-start | bytes 1572872 | tf_op jit(solution)/shard_map/ppermute | solution.py:38
  84.3 17.5 %copy-start = (bf16[1024,1408]{1,0:T(8,128)(2,1)S(1)}, bf16[1024,1408]{1,0:T(8,128)(2,1)}, u32[]{:S(2)}) copy-start(bf16[1024,1408]{1,0:T(8,128)(2,1)} %get-tuple-element.44) | copy-start | bytes 8650756
  84.4 0.8 copy-start.2
  91.4 2.8 %collective-permute-start.22 = (f32[2,1024]{1,0:T(2,128)}, f32[2,1024]{1,0:T(2,128)S(1)}, u32[]{:S(2)}, u32[]{:S(2)}) collective-permute-start(f32[2,1024]{1,0:T(2,128)} %get-tuple-element.36), channel_id=1, source_target_pairs={{64,0},{72,8},{65,1},{73,9},{66,2},{74,10},{67,3},{75,11},{80,16},... | collective-permute-start | bytes 24584 | tf_op jit(solution)/shard_map/ppermute | solution.py:38
  91.7 3.2 %collective-permute-start.23 = (f32[16,256]{1,0:T(8,128)}, f32[16,256]{1,0:T(8,128)S(1)}, u32[]{:S(2)}, u32[]{:S(2)}) collective-permute-start(f32[16,256]{1,0:T(8,128)} %get-tuple-element.37), channel_id=1, source_target_pairs={{8,0},{0,8},{9,1},{1,9},{10,2},{2,10},{11,3},{3,11},{24,16},{16,24... | collective-permute-start | bytes 49160 | tf_op jit(solution)/shard_map/ppermute | solution.py:38
  95.7 2.7 %collective-permute-start.24 = (f32[2,1024]{1,0:T(2,128)S(1)}, f32[2,1024]{1,0:T(2,128)S(1)}, u32[]{:S(2)}, u32[]{:S(2)}) collective-permute-start(f32[2,1024]{1,0:T(2,128)S(1)} %multiply_add_fusion.6), channel_id=1, source_target_pairs={{1,0},{9,8},{2,1},{10,9},{3,2},{11,10},{0,3},{8,11},{17,16},{25,24... | collective-permute-start | bytes 24584 | tf_op jit(solution)/shard_map/ppermute | solution.py:38
  97.7 3.8 %collective-permute-start.25 = (f32[16,256]{1,0:T(8,128)S(1)}, f32[16,256]{1,0:T(8,128)S(1)}, u32[]{:S(2)}, u32[]{:S(2)}) collective-permute-start(f32[16,256]{1,0:T(8,128)S(1)} %multiply_add_fusion.3), channel_id=1, source_target_pairs={{68,0},{76,8},{69,1},{77,9},{70,2},{78,10},{71,3},{79,11},{84,16},... | collective-permute-start | bytes 49160 | tf_op jit(solution)/shard_map/ppermute | solution.py:38
  101.5 4.3 %collective-permute-start.26 = (f32[2,1024]{1,0:T(2,128)S(1)}, f32[2,1024]{1,0:T(2,128)S(1)}, u32[]{:S(2)}, u32[]{:S(2)}) collective-permute-start(f32[2,1024]{1,0:T(2,128)S(1)} %multiply_add_fusion.5), channel_id=1, source_target_pairs={{2,0},{10,8},{3,1},{11,9},{0,2},{8,10},{1,3},{9,11},{18,16},{26,24... | collective-permute-start | bytes 24584 | tf_op jit(solution)/shard_map/ppermute | solution.py:38
  104.7 2.6 %collective-permute-start.27 = (f32[16,256]{1,0:T(8,128)S(1)}, f32[16,256]{1,0:T(8,128)S(1)}, u32[]{:S(2)}, u32[]{:S(2)}) collective-permute-start(f32[16,256]{1,0:T(8,128)S(1)} %multiply_add_fusion.2), channel_id=1, source_target_pairs={{16,0},{24,8},{17,1},{25,9},{18,2},{26,10},{19,3},{27,11},{32,16},... | collective-permute-start | bytes 49160 | tf_op jit(solution)/shard_map/ppermute | solution.py:38
  107.4 4.2 %collective-permute-start.28 = (f32[16,256]{1,0:T(8,128)S(1)}, f32[16,256]{1,0:T(8,128)S(1)}, u32[]{:S(2)}, u32[]{:S(2)}) collective-permute-start(f32[16,256]{1,0:T(8,128)S(1)} %multiply_add_fusion.1), channel_id=1, source_target_pairs={{32,0},{40,8},{33,1},{41,9},{34,2},{42,10},{35,3},{43,11},{48,16},... | collective-permute-start | bytes 49160 | tf_op jit(solution)/shard_map/ppermute | solution.py:38
  142.8 10.2 %collective-permute-start.29 = (f32[64,88,128]{2,1,0:T(8,128)}, f32[64,88,128]{2,1,0:T(8,128)S(1)}, u32[]{:S(2)}, u32[]{:S(2)}) collective-permute-start(f32[64,88,128]{2,1,0:T(8,128)} %get-tuple-element.46), channel_id=1, source_target_pairs={{8,0},{0,8},{9,1},{1,9},{10,2},{2,10},{11,3},{3,11},{24,16},{16,24... | collective-permute-start | bytes 8650760 | tf_op jit(solution)/shard_map/ppermute | solution.py:38
  156.6 44.6 %all-to-all-start = ((f32[64,88,128]{2,1,0:T(8,128)}), f32[64,88,128]{2,1,0:T(8,128)S(1)}, u32[]{:S(2)}, u32[]{:S(2)}) async-start(f32[64,88,128]{2,1,0:T(8,128)} %add.64), calls=%async_computation | async-start | bytes 5767168 | tf_op jit(solution)/shard_map/all_to_all | solution.py:481
  232.9 6.7 %collective-permute-start.30 = (f16[64,96,128]{2,1,0:T(8,128)(2,1)S(1)}, f16[64,96,128]{2,1,0:T(8,128)(2,1)S(1)}, u32[]{:S(2)}, u32[]{:S(2)}) collective-permute-start(f16[64,96,128]{2,1,0:T(8,128)(2,1)S(1)} %all_to_all.10), channel_id=1, source_target_pairs={{8,0},{0,8},{9,1},{1,9},{10,2},{2,10},{11,3},{3,11},{24,16},{16,24... | collective-permute-start | bytes 4718600 | tf_op jit(solution)/shard_map/ppermute | solution.py:38
where the time goes:
time: 246 us; the launch traced here: 245 us
  Pallas kernels  73.3 us (30%)
  waiting for transfers between devices  66.8 us (27%)
  starting transfers between devices  54.7 us (22%)
  blocking collectives  29.7 us (12%)
  other arithmetic  9.47 us (4%)
  local copies, waits for them, and re-layouts  5.61 us (2%)
  between operations  5.56 us (2%)
    ppermute x31, starting transfers between devices, take_from(): return lax.ppermute(value, AXES, perm)  46.7 us
    all_to_all x1, waiting for transfers between devices, swap_blocks(): lax.all_to_all(value, AXES, split_axis=0, concat_axis=0, axis_index_group...  34 us
    ppermute x31, waiting for transfers between devices, take_from(): return lax.ppermute(value, AXES, perm)  32.8 us
    pallas_call x1, Pallas kernels, grad_of(): pl.pallas_call(grad_kernel, grid=(rows // step,), out_shape=(piece, piece...  30.5 us
    all_to_all x1, blocking collectives, swap_blocks(): lax.all_to_all(value, AXES, split_axis=0, concat_axis=0, axis_index_group...  29.7 us
    pallas_call x3, Pallas kernels, logits_of(): pl.pallas_call(functools.partial(logits_kernel, count, first, last), out_...  28.8 us
    pallas_call x1, Pallas kernels, project(): pl.pallas_call(proj_kernel, grid=(2,), out_shape=(jax.ShapeDtypeStruct((2...  8.64 us
    all_to_all x1, starting transfers between devices, swap_blocks(): lax.all_to_all(value, AXES, split_axis=0, concat_axis=0, axis_index_group...  7.99 us
  transfers between devices with their start and end apart: 32, of which 16 were waited for; matrix products, arithmetic and copies ran while one was open for 2% of the time, Pallas kernels for 14%

commit v1 on v0

--- a/solution.py
+++ b/solution.py
@@ -17,7 +17,7 @@
 WIDE = 2 * LANES
 BATCHES = (((0, 0), (1, 0), (0, 1), (0, 3)), ((1, 3), (0, 2), (1, 1)), ((1, 2),))
 ORDER = [(core,) + place for batch in BATCHES for core in range(2) for place in batch]
-POINT_ORDER = tuple(range(8))
+POINT_ORDER = (0, 1, 3, 4, 2, 5, 7, 6)
 
 
 def device_index(x, y, z, core):
@@ -95,47 +95,71 @@
 
 
 def proj_kernel(*refs):
-    feature_refs = refs[:8]
-    weight_ref, tile_ref, proj_ref, unit_ref = refs[8:]
-    step = pl.program_id(0)
+    feature_refs = refs[:4]
+    weight_ref = refs[4]
+    outs, (tile_ref, weight_in_ref, proj_ref, unit_ref, in_sem, out_sem) = refs[-9:-6], refs[-6:]
+    base = 0 if len(refs) == 14 else tile_ref.shape[0]
     rows = feature_refs[0].shape[0]
-    for turn in range(2):
-
-        @pl.when(step == turn)
-        def _():
-            for k in range(4):
-                tile_ref[k * rows : (k + 1) * rows, :] = feature_refs[4 * turn + k][...]
-
-    proj = jnp.dot(tile_ref[...], weight_ref[...], preferred_element_type=jnp.float32)
-    inv = lax.rsqrt(jnp.sum(proj * proj, axis=-1, keepdims=True) + EPS)
-    proj_ref[...] = proj
-    unit_ref[...] = (proj * inv).astype(jnp.bfloat16)
-
-
-def project(features, weight):
+    step = 2 * rows
+    incoming = [pltpu.make_async_copy(weight_ref, weight_in_ref, in_sem.at[4])]
+    for k in range(4):
+        to = tile_ref.at[k * rows : (k + 1) * rows, :]
+        incoming.append(pltpu.make_async_copy(feature_refs[k], to, in_sem.at[k]))
+    for copy in incoming:
+        copy.start()
+    for copy in incoming:
+        copy.wait()
+    outgoing = []
+
+    def send(held_ref, out_ref, at, count):
+        copy = pltpu.make_async_copy(
+            held_ref.at[at : at + count, :],
+            out_ref.at[base + at : base + at + count, :],
+            out_sem.at[len(outgoing)],
+        )
+        copy.start()
+        outgoing.append(copy)
+
+    send(tile_ref, outs[0], 0, 2 * step)
+    for at in range(0, 2 * step, step):
+        proj = jnp.dot(
+            tile_ref[at : at + step, :], weight_in_ref[...], preferred_element_type=jnp.float32
+        )
+        inv = lax.rsqrt(jnp.sum(proj * proj, axis=-1, keepdims=True) + EPS)
+        proj_ref[at : at + step, :] = proj
+        unit_ref[at : at + step, :] = (proj * inv).astype(jnp.bfloat16)
+        send(proj_ref, outs[1], at, step)
+        send(unit_ref, outs[2], at, step)
+    for copy in outgoing:
+        copy.wait()
+
+
+def project(features, weight, done):
     deep, width = weight.shape
-    step = 4 * features[0].shape[0]
-    once = pl.Buffered(1)
-
-    def rows_of(array_width):
-        return pl.BlockSpec((step, array_width), lambda i: (i, 0))
-
+    rows = 4 * features[0].shape[0]
     return pl.pallas_call(
         proj_kernel,
-        grid=(2,),
         out_shape=(
-            jax.ShapeDtypeStruct((2 * step, deep), jnp.bfloat16),
-            jax.ShapeDtypeStruct((2 * step, width), jnp.float32),
-            jax.ShapeDtypeStruct((2 * step, width), jnp.bfloat16),
+            jax.ShapeDtypeStruct((2 * rows, deep), jnp.bfloat16),
+            jax.ShapeDtypeStruct((2 * rows, width), jnp.float32),
+            jax.ShapeDtypeStruct((2 * rows, width), jnp.bfloat16),
         ),
-        in_specs=[pl.BlockSpec(part.shape, lambda i: (0, 0), pipeline_mode=once) for part in features]
-        + [pl.BlockSpec((deep, width), lambda i: (0, 0), pipeline_mode=once)],
-        out_specs=(rows_of(deep), rows_of(width), rows_of(width)),
-        compiler_params=params(58, True),
+        in_specs=[anywhere()] * (5 + len(done)),
+        out_specs=(anywhere(), anywhere(), anywhere()),
+        input_output_aliases={5 + k: k for k in range(len(done))},
+        scratch_shapes=[
+            pltpu.VMEM((rows, deep), jnp.bfloat16),
+            pltpu.VMEM((deep, width), jnp.bfloat16),
+            pltpu.VMEM((rows, width), jnp.float32),
+            pltpu.VMEM((rows, width), jnp.bfloat16),
+            pltpu.SemaphoreType.DMA((5,)),
+            pltpu.SemaphoreType.DMA((5,)),
+        ],
+        compiler_params=params(58),
         cost_estimate=pl.CostEstimate(
-            flops=4 * step * deep * width, bytes_accessed=12 * 2**20, transcendentals=0
+            flops=2 * rows * deep * width, bytes_accessed=6 * 2**20, transcendentals=0
         ),
-    )(*features, weight)
+    )(*features, weight, *done)
 
 
 def to_column(row):
@@ -155,8 +179,8 @@
         old_max_ref, old_sum_ref = refs[:2]
         refs = refs[2:]
     if last:
-        old_col_refs = refs[:2]
-        refs = refs[2:]
+        old_col_refs = refs[:1]
+        refs = refs[1:]
     logits_ref, col_ref = refs[:2]
     refs = refs[2:]
     if first:
@@ -230,7 +254,8 @@
                 part = row_sum_ref[r : r + LANES, lanes].T
                 top = jnp.max(tops, axis=0, keepdims=True)
                 total = jnp.sum(part * jnp.exp2(tops - top), axis=0, keepdims=True)
-                row_ref[which : which + 1, r : r + LANES] = top + jnp.log(total) * LOG2E
+                to = POINT_ORDER[r // LANES] * LANES
+                row_ref[which : which + 1, to : to + LANES] = top + jnp.log(total) * LOG2E
     for j in range(count):
         copy_out(j).wait()
 
@@ -274,11 +299,11 @@
 
 
 def grad_kernel(place_ref, scale_ref, *refs):
-    logits_refs = refs[:3]
-    target_refs = refs[3:19]
-    row_ref, all_col_ref, diag_ref, proj_ref, turned_any, kept_ref, sent_ref, loss_ref = refs[19:27]
-    coef_ref, targets_ref, tops_ref, shares_ref, edges_ref, high_ref, low_ref = refs[27:34]
-    part_ref, turned_ref, sem_ref = refs[34:]
+    logits_refs = refs[:2]
+    target_refs = refs[2:18]
+    row_ref, all_col_ref, diag_ref, proj_ref, turned_any, kept_ref, sent_ref, loss_ref = refs[18:26]
+    coef_ref, targets_ref, tops_ref, shares_ref, edges_ref, high_ref, low_ref = refs[26:33]
+    part_ref, turned_ref, sem_ref = refs[33:]
     step = pl.program_id(0)
     size = proj_ref.shape[0]
     scale = scale_ref[0]
@@ -296,7 +321,7 @@
 
     @pl.when(step == 0)
     def _():
-        for k in range(17):
+        for k in range(16):
             copy_in(k).start()
         for k, block in enumerate(ORDER):
             at = canonical(block)
@@ -311,6 +336,10 @@
         both = edges_ref[:1, :] - 2.0 * diag_ref[:1, :]
         both = both[:, :LANES] + both[:, LANES:] + row_ref[:1, :LANES] + row_ref[1:2, :LANES]
         loss_ref[...] = jnp.broadcast_to(both, loss_ref.shape)
+
+    @pl.when(step == 1)
+    def _():
+        copy_in(16).start()
 
     def own_hits(r):
         rows_at = lax.broadcasted_iota(jnp.int32, (chunk, WIDE), 0) + r + step * size
@@ -516,29 +545,36 @@
     return rows, col_add(cols, jnp.roll(got_cols.reshape(col_shape), 2, axis=2))
 
 
-def gather_points(own):
-    def near(value):
+def gather_and_project(own_points, own_targets, weight):
+    def near_point(value):
         return take_from(value, x_map=X_POINT)
 
-    beside, after, before = near(own), take_from(own, dz=1), take_from(own, dz=-1)
-    beside_before, far, beside_after = take_from(beside, dz=-1), take_from(after, dz=1), near(after)
+    def near_target(value):
+        return take_from(value, x_map=X_TARGET)
+
+    own = own_points
+    beside, after, before = near_point(own), take_from(own, dz=1), take_from(own, dz=-1)
+    target = own_targets
+    near = [own, after, before, beside]
+    beside_after, far = near_point(after), take_from(after, dz=1)
+    beside_before = take_from(beside, dz=-1)
+    t_beside, t_after = near_target(target), take_from(target, dy=1)
+
+    t_before = take_from(target, dy=-1)
     beside_far = take_from(beside_after, dz=1)
-    return [own, after, far, before, beside, beside_after, beside_far, beside_before]
-
-
-def gather_targets(own):
-    def near(value):
-        return take_from(value, x_map=X_TARGET)
-
-    def with_other(blocks):
-        return blocks + [take_from(block, flip=1) for block in blocks]
-
-    beside, after, before = near(own), take_from(own, dy=1), take_from(own, dy=-1)
-    first = with_other([own, beside, after, before])
-    beside_before, far, beside_after = take_from(beside, dy=-1), take_from(after, dy=1), near(after)
-    second = with_other([beside_before, far, beside_after])
-    third = with_other([take_from(beside_after, dy=1)])
-    return [first, second, third]
+    half = project(near, weight, ())
+    t_beside, t_after, far, beside_before, beside_far, half = lax.optimization_barrier(
+        (t_beside, t_after, far, beside_before, beside_far, half)
+    )
+    t_beside_after, t_far = near_target(t_after), take_from(t_after, dy=1)
+    t_beside_before = take_from(t_beside, dy=-1)
+    points = project([far, beside_after, beside_before, beside_far], weight, half)
+    first = [target, t_beside, t_after, t_before]
+    return points, first, [t_beside_before, t_far, t_beside_after]
+
+
+def with_other(blocks):
+    return blocks + [take_from(block, flip=1) for block in blocks]
 
 
 def total_sum(place, kept, sent, local_loss):
@@ -568,20 +604,22 @@
     place = (lax.axis_index("row") % 2).astype(jnp.int32).reshape(1)
 
     own = unit_targets(image_vals, image_scales, text_vals, text_scales)
-    targets = gather_targets(own)
-    tile, proj, points = project(gather_points(features), proj_weight)
+    (tile, proj, points), near, far = gather_and_project(features, own, proj_weight)
     turned = tile.T
-    first, near_cols, diag, *old = logits_of(points, logit_scale, targets[0], (), ())
-    second, far_cols, *old = logits_of(points, logit_scale, targets[1], old, ())
-    third, _, rows_part, cols_part = logits_of(
-        points, logit_scale, targets[2], old, (near_cols, far_cols)
-    )
+    near = with_other(near)
+    beside_after, points = lax.optimization_barrier((far[-1], points))
+    last = take_from(beside_after, dy=1)
+    far = with_other(far)
+    first, near_cols, diag, *old = logits_of(points, logit_scale, near, (), ())
+    last, near_cols = lax.optimization_barrier((last, near_cols))
+    far = far + with_other([last])
+    second, _, rows_part, cols_part = logits_of(points, logit_scale, far, old, (near_cols,))
     row_lse, col_lse = exchange_statistics(rows_part, cols_part)
     kept, sent, losses = grad_of(
         place,
         logit_scale,
-        (first, second, third),
-        sum(targets, []),
+        (first, second),
+        near + far,
         row_lse,
         col_lse,
         diag,

time: 246 us -> 250 us (1.016)
  starting transfers between devices: 54.7 us -> 63.6 us
  waiting for transfers between devices: 66.8 us -> 63 us
    ppermute x31, starting transfers between devices: 46.7 us -> 54.1 us  [take_from(): return lax.ppermute(value, AXES, perm)]
    pallas_call x3 -> x2, Pallas kernels: 28.8 us -> 24.8 us  [logits_of(): pl.pallas_call(functools.partial(logits_kernel, count, first, last), out_...]
    ppermute x31, waiting for transfers between devices: 32.8 us -> 29.1 us  [take_from(): return lax.ppermute(value, AXES, perm)]
    pallas_call x1 -> x2, Pallas kernels: 8.64 us -> 10.4 us  [project(): pl.pallas_call(proj_kernel, out_shape=(jax.ShapeDtypeStruct((2 * rows, de...]
  transfers between devices with their start and end apart: 32 -> 32, of which waited for: 16 -> 12; matrix products, arithmetic and copies ran while one was open for 2% -> 2% of each run, Pallas kernels for 14% -> 10%
where the time goes in v1:
time: 250 us; the launch traced here: 249 us
  Pallas kernels  71.2 us (28%)
  starting transfers between devices  63.6 us (25%)
  waiting for transfers between devices  63 us (25%)
  blocking collectives  29.7 us (12%)
  other arithmetic  9.5 us (4%)
  local copies, waits for them, and re-layouts  6.88 us (3%)
  between operations  5.68 us (2%)
    ppermute x31, starting transfers between devices, take_from(): return lax.ppermute(value, AXES, perm)  54.1 us
    all_to_all x1, waiting for transfers between devices, swap_blocks(): lax.all_to_all(value, AXES, split_axis=0, concat_axis=0, axis_index_group...  33.8 us
    pallas_call x1, Pallas kernels, grad_of(): pl.pallas_call(grad_kernel, grid=(rows // step,), out_shape=(piece, piece...  30.6 us
    all_to_all x1, blocking collectives, swap_blocks(): lax.all_to_all(value, AXES, split_axis=0, concat_axis=0, axis_index_group...  29.7 us
    ppermute x31, waiting for transfers between devices, take_from(): return lax.ppermute(value, AXES, perm)  29.1 us
    pallas_call x2, Pallas kernels, logits_of(): pl.pallas_call(functools.partial(logits_kernel, count, first, last), out_...  24.8 us
    pallas_call x2, Pallas kernels, project(): pl.pallas_call(proj_kernel, out_shape=(jax.ShapeDtypeStruct((2 * rows, de...  10.4 us
    all_to_all x1, starting transfers between devices, swap_blocks(): lax.all_to_all(value, AXES, split_axis=0, concat_axis=0, axis_index_group...  9.5 us
  transfers between devices with their start and end apart: 32, of which 12 were waited for; matrix products, arithmetic and copies ran while one was open for 2% of the time, Pallas kernels for 10%

profile of v1, /device:TPU:1, one launch (start us, length us, event | category | flops | bytes accessed | tf_op | source)
XLA Modules:
  0.0 249.5 jit_solution(16551781453782453617)
XLA Ops:
  0.6 4.7 %collective-permute-start.2 = (bf16[128,1408]{1,0:T(8,128)(2,1)}, bf16[128,1408]{1,0:T(8,128)(2,1)S(1)}, u32[]{:S(2)}, u32[]{:S(2)}) collective-permute-start(bf16[128,1408]{1,0:T(8,128)(2,1)} %refs_0_.3), channel_id=1, source_target_pairs={{1,0},{9,8},{2,1},{10,9},{3,2},{11,10},{0,3},{8,11},{17,16},{25,24... | collective-permute-start | bytes 1081352 | tf_op jit(solution)/shard_map/ppermute | solution.py:38
  5.3 1.2 collective-permute-start.4
  6.5 6.2 %collective-permute-done.2.refs_1_ = bf16[128,1408]{1,0:T(8,128)(2,1)S(1)} collective-permute-done((bf16[128,1408]{1,0:T(8,128)(2,1)}, bf16[128,1408]{1,0:T(8,128)(2,1)S(1)}, u32[]{:S(2)}, u32[]{:S(2)}) %collective-permute-start.2) | collective-permute-done | bytes 360480 | tf_op jit(solution)/shard_map/ppermute | solution.py:38
  12.7 1.2 collective-permute-start.6
  13.9 2.6 %shard_map.86.refs_2_ = bf16[256,1024]{1,0:T(8,128)(2,1)} custom-call(bf16[128,1024]{1,0:T(8,128)(2,1)} %image_ref.1, bf16[8,128]{1,0:T(8,128)(2,1)} %bitcast.14, bf16[128,1024]{1,0:T(8,128)(2,1)} %text_ref.1, bf16[8,128]{1,0:T(8,128)(2,1)} %bitcast.15), custom_call_target="tpu_custom_call" | custom-call | flops 1048576 | bytes 1048576 | tf_op jit(solution)/shard_map/pallas_call | solution.py:87
  16.5 2.7 %collective-permute-start.1 = (bf16[256,1024]{1,0:T(8,128)(2,1)}, bf16[256,1024]{1,0:T(8,128)(2,1)S(1)}, u32[]{:S(2)}, u32[]{:S(2)}) collective-permute-start(bf16[256,1024]{1,0:T(8,128)(2,1)} %shard_map.86.refs_2_), channel_id=1, source_target_pairs={{16,0},{24,8},{17,1},{25,9},{18,2},{26,10},{19,3},{27,11},{32,16},... | collective-permute-start | bytes 1572872 | tf_op jit(solution)/shard_map/ppermute | solution.py:38
  19.2 1.8 collective-permute-start
  21.0 3.3 %collective-permute-start.3 = (bf16[128,1408]{1,0:T(8,128)(2,1)S(1)}, bf16[128,1408]{1,0:T(8,128)(2,1)S(1)}, u32[]{:S(2)}, u32[]{:S(2)}) collective-permute-start(bf16[128,1408]{1,0:T(8,128)(2,1)S(1)} %collective-permute-done.2.refs_1_), channel_id=1, source_target_pairs={{1,0},{9,8},{2,1},{10,9},{3,2},{11,10},{0,3},{8,11},{17,16},{25,24... | collective-permute-start | bytes 1081352 | tf_op jit(solution)/shard_map/ppermute | solution.py:38
  24.3 2.7 %collective-permute-start.7 = (bf16[128,1408]{1,0:T(8,128)(2,1)S(1)}, bf16[128,1408]{1,0:T(8,128)(2,1)S(1)}, u32[]{:S(2)}, u32[]{:S(2)}) collective-permute-start(bf16[128,1408]{1,0:T(8,128)(2,1)S(1)} %collective-permute-done.6.refs_1_), channel_id=1, source_target_pairs={{1,0},{9,8},{2,1},{10,9},{3,2},{11,10},{0,3},{8,11},{17,16},{25,24... | collective-permute-start | bytes 1081352 | tf_op jit(solution)/shard_map/ppermute | solution.py:38
  27.0 1.9 collective-permute-done.1.refs_4_
  28.9 0.7 collective-permute-start.10
  29.6 5.2 %shard_map.87 = (bf16[1024,1408]{1,0:T(8,128)(2,1)}, f32[1024,1024]{1,0:T(8,128)}, bf16[1024,1024]{1,0:T(8,128)(2,1)}) custom-call(bf16[128,1408]{1,0:T(8,128)(2,1)} %refs_0_.3, bf16[128,1408]{1,0:T(8,128)(2,1)} %copy-done.21, bf16[128,1408]{1,0:T(8,128)(2,1)} %copy-done.23, bf16[128,1408]{1,0:T(8,128)(2,1)} %copy-done.22, bf16[1408,1024]{1,0:T(8,128)(2,1)} %refs_4_.3), custom_call_target="tpu_custom_call" | custom-call | flops 1476395008 | bytes 6291456 | tf_op jit(solution)/shard_map/pallas_call | solution.py:140
  34.8 3.1 %collective-permute-start.11 = (bf16[256,1024]{1,0:T(8,128)(2,1)S(1)}, bf16[256,1024]{1,0:T(8,128)(2,1)S(1)}, u32[]{:S(2)}, u32[]{:S(2)}) collective-permute-start(bf16[256,1024]{1,0:T(8,128)(2,1)S(1)} %copy-done.1), channel_id=1, source_target_pairs={{8,0},{0,8},{9,1},{1,9},{10,2},{2,10},{11,3},{3,11},{24,16},{16,24... | collective-permute-start | bytes 1572872 | tf_op jit(solution)/shard_map/ppermute | solution.py:38
  38.0 0.9 copy-done.19
  38.8 1.8 collective-permute-start.9
  40.6 1.3 collective-permute-done.10.refs_5_
  41.9 3.4 %collective-permute-start.14 = (bf16[256,1024]{1,0:T(8,128)(2,1)S(1)}, bf16[256,1024]{1,0:T(8,128)(2,1)S(1)}, u32[]{:S(2)}, u32[]{:S(2)}) collective-permute-start(bf16[256,1024]{1,0:T(8,128)(2,1)S(1)} %collective-permute-done.10.refs_5_), channel_id=1, source_target_pairs={{8,0},{0,8},{9,1},{1,9},{10,2},{2,10},{11,3},{3,11},{24,16},{16,24... | collective-permute-start | bytes 1572872 | tf_op jit(solution)/shard_map/ppermute | solution.py:38
  45.4 2.9 %collective-permute-start.16 = (bf16[256,1024]{1,0:T(8,128)(2,1)S(1)}, bf16[256,1024]{1,0:T(8,128)(2,1)S(1)}, u32[]{:S(2)}, u32[]{:S(2)}) collective-permute-start(bf16[256,1024]{1,0:T(8,128)(2,1)S(1)} %collective-permute-done.1.refs_4_), channel_id=1, source_target_pairs={{16,0},{24,8},{17,1},{25,9},{18,2},{26,10},{19,3},{27,11},{32,16},... | collective-permute-start | bytes 1572872 | tf_op jit(solution)/shard_map/ppermute | solution.py:38
  48.3 2.6 %collective-permute-done.9.refs_4_.refs_12_ = bf16[256,1024]{1,0:T(8,128)(2,1)S(1)} collective-permute-done((bf16[256,1024]{1,0:T(8,128)(2,1)S(1)}, bf16[256,1024]{1,0:T(8,128)(2,1)S(1)}, u32[]{:S(2)}, u32[]{:S(2)}) %collective-permute-start.9) | collective-permute-done | bytes 524320 | tf_op jit(solution)/shard_map/ppermute | solution.py:38
  50.9 3.5 %collective-permute-start.13 = (bf16[256,1024]{1,0:T(8,128)(2,1)S(1)}, bf16[256,1024]{1,0:T(8,128)(2,1)S(1)}, u32[]{:S(2)}, u32[]{:S(2)}) collective-permute-start(bf16[256,1024]{1,0:T(8,128)(2,1)S(1)} %collective-permute-done.1.refs_4_), channel_id=1, source_target_pairs={{8,0},{0,8},{9,1},{1,9},{10,2},{2,10},{11,3},{3,11},{24,16},{16,24... | collective-permute-start | bytes 1572872 | tf_op jit(solution)/shard_map/ppermute | solution.py:38
  54.4 5.2 %shard_map.88 = (bf16[1024,1408]{1,0:T(8,128)(2,1)}, f32[1024,1024]{1,0:T(8,128)}, bf16[1024,1024]{1,0:T(8,128)(2,1)}) custom-call(bf16[128,1408]{1,0:T(8,128)(2,1)} %copy-done.18, bf16[128,1408]{1,0:T(8,128)(2,1)} %copy-done.17, bf16[128,1408]{1,0:T(8,128)(2,1)} %copy-done.19, ...), custom_call_target="tpu_custom_call", output_to_operand_aliasing={{0}: (5, {}), {1}: (6, {}), {2}: (7, {})} | custom-call | flops 1476395008 | bytes 6291456 | tf_op jit(solution)/shard_map/pallas_call | solution.py:140
  59.7 2.6 %collective-permute-start.20 = (bf16[256,1024]{1,0:T(8,128)(2,1)S(1)}, bf16[256,1024]{1,0:T(8,128)(2,1)S(1)}, u32[]{:S(2)}, u32[]{:S(2)}) collective-permute-start(bf16[256,1024]{1,0:T(8,128)(2,1)S(1)} %collective-permute-done.9.refs_4_.refs_12_), channel_id=1, source_target_pairs={{16,0},{24,8},{17,1},{25,9},{18,2},{26,10},{19,3},{27,11},{32,16},... | collective-permute-start | bytes 1572872 | tf_op jit(solution)/shard_map/ppermute | solution.py:38
  63.0 0.6 collective-permute-start.19
  63.6 0.1 collective-permute-start.17
  63.7 0.4 collective-permute-start.18
  64.1 0.3 copy-done.9
  64.4 0.8 copy-done.11
  65.2 12.0 %shard_map.89 = (f32[1024,2048]{1,0:T(8,128)}, f32[8,256]{1,0:T(8,128)}, f32[8,256]{1,0:T(8,128)}, f32[1024,256]{1,0:T(8,128)}, f32[1024,256]{1,0:T(8,128)}) custom-call(f32[1]{0:T(128)S(6)} %copy.16.refs_0_.scale_ref, bf16[1024,1024]{1,0:T(8,128)(2,1)} %get-tuple-element.48.refs_1_, bf16[256,1024]{1,0:T(8,128)(2,1)} %shard_map.86.refs_2_, ...), custom_call_target="tpu_custom_call" | custom-call | flops 4294967296 | bytes 8388608 | tf_op jit(solution)/shard_map/pallas_call | solution.py:281
  77.2 0.1 collective-permute-start.21
  77.4 1.8 collective-permute-done.21.refs_9_.refs_17_
  79.2 0.8 copy-done.16
  80.1 12.8 %shard_map.90 = (f32[1024,2048]{1,0:T(8,128)}, f32[8,256]{1,0:T(8,128)}, f32[2,1024]{1,0:T(2,128)}, f32[16,256]{1,0:T(8,128)}) custom-call(f32[1]{0:T(128)S(6)} %copy.16.refs_0_.scale_ref, bf16[1024,1024]{1,0:T(8,128)(2,1)} %get-tuple-element.48.refs_1_, bf16[256,1024]{1,0:T(8,128)(2,1)} %copy-done.8, bf16[256,1024]{1,0:T(8,128)(2,1)} %copy-done.10, ...), custom_call_target="tpu_custom_call" | custom-call | flops 4294967296 | bytes 8388608 | tf_op jit(solution)/shard_map/pallas_call | solution.py:281
  92.9 0.2 collective-permute-start.23
  93.1 2.5 %collective-permute-done.22 = f32[2,1024]{1,0:T(2,128)S(1)} collective-permute-done((f32[2,1024]{1,0:T(2,128)}, f32[2,1024]{1,0:T(2,128)S(1)}, u32[]{:S(2)}, u32[]{:S(2)}) %collective-permute-start.22) | collective-permute-done | bytes 8224 | tf_op jit(solution)/shard_map/ppermute | solution.py:38
  95.7 0.7 multiply_add_fusion.6
  96.5 0.7 multiply_add_fusion.3
  97.2 3.4 %collective-permute-start.24 = (f32[2,1024]{1,0:T(2,128)S(1)}, f32[2,1024]{1,0:T(2,128)S(1)}, u32[]{:S(2)}, u32[]{:S(2)}) collective-permute-start(f32[2,1024]{1,0:T(2,128)S(1)} %multiply_add_fusion.6), channel_id=1, source_target_pairs={{1,0},{9,8},{2,1},{10,9},{3,2},{11,10},{0,3},{8,11},{17,16},{25,24... | collective-permute-start | bytes 24584 | tf_op jit(solution)/shard_map/ppermute | solution.py:38
  100.6 1.8 collective-permute-start.25
  102.5 1.9 collective-permute-done.25
  104.5 2.9 %copy.12 = bf16[1024,1408]{0,1:T(8,128)(2,1)} copy(bf16[1024,1408]{1,0:T(8,128)(2,1)S(1)} %copy-done) | data formatting | bytes 5767168 | tf_op jit(solution)/shard_map/pallas_call | solution.py:140
  107.4 1.5 collective-permute-start.27
  109.0 1.0 collective-permute-done.27
  110.1 1.3 collective-permute-start.28
  111.4 0.6 multiply_add_fusion.4.refs_18_
  112.0 2.2 collective-permute-done.28
  114.3 0.6 multiply_add_fusion.refs_19_
  114.9 30.6 %shard_map.91 = (f32[64,88,128]{2,1,0:T(8,128)}, f32[64,88,128]{2,1,0:T(8,128)}, f32[8,128]{1,0:T(8,128)}) custom-call(s32[1]{0:T(128)} %bitcast.place_ref, f32[1]{0:T(128)S(6)} %copy.16.refs_0_.scale_ref, f32[1024,2048]{1,0:T(8,128)} %get-tuple-element.50.refs_0_, f32[1024,2048]{1,0:T(8,128)} %get-tuple-element.57.refs_1_, ...), custom_call_target="tpu_custom_call" | custom-call | flops 8589934592 | bytes 33554432 | tf_op jit(solution)/shard_map/pallas_call | solution.py:422
  145.6 5.1 %collective-permute-start.29 = (f32[64,88,128]{2,1,0:T(8,128)}, f32[64,88,128]{2,1,0:T(8,128)S(1)}, u32[]{:S(2)}, u32[]{:S(2)}) collective-permute-start(f32[64,88,128]{2,1,0:T(8,128)} %get-tuple-element.68), channel_id=1, source_target_pairs={{8,0},{0,8},{9,1},{1,9},{10,2},{2,10},{11,3},{3,11},{24,16},{16,24... | collective-permute-start | bytes 8650760 | tf_op jit(solution)/shard_map/ppermute | solution.py:38
  150.7 5.1 %collective-permute-done.29 = f32[64,88,128]{2,1,0:T(8,128)S(1)} collective-permute-done((f32[64,88,128]{2,1,0:T(8,128)}, f32[64,88,128]{2,1,0:T(8,128)S(1)}, u32[]{:S(2)}, u32[]{:S(2)}) %collective-permute-start.29) | collective-permute-done | bytes 2883616 | tf_op jit(solution)/shard_map/ppermute | solution.py:38
  155.8 3.7 %add.64 = f32[64,88,128]{2,1,0:T(8,128)} add(f32[64,88,128]{2,1,0:T(8,128)} %get-tuple-element.67, f32[64,88,128]{2,1,0:T(8,128)S(1)} %collective-permute-done.29) | non-fusion elementwise | flops 720896 | bytes 8650752 | tf_op jit(solution)/shard_map/add | solution.py:582
  159.5 9.5 %all-to-all-start = ((f32[64,88,128]{2,1,0:T(8,128)}), f32[64,88,128]{2,1,0:T(8,128)S(1)}, u32[]{:S(2)}, u32[]{:S(2)}) async-start(f32[64,88,128]{2,1,0:T(8,128)} %add.64), calls=%async_computation | async-start | bytes 5767168 | tf_op jit(solution)/shard_map/all_to_all | solution.py:510
  169.0 1.3 slice_reduce_fusion
  171.7 33.8 %all-to-all-done = f32[64,88,128]{2,1,0:T(8,128)S(1)} async-done(((f32[64,88,128]{2,1,0:T(8,128)}), f32[64,88,128]{2,1,0:T(8,128)S(1)}, u32[]{:S(2)}, u32[]{:S(2)}) %all-to-all-start) | async-done | bytes 2883616 | tf_op jit(solution)/shard_map/all_to_all | solution.py:510
  205.6 0.2 reduce_sum.18
  205.8 0.6 abs_reduce_fusion
  207.1 0.1 stack.23
  207.4 0.2 broadcast_in_dim.10
  207.6 29.7 %all_to_all.10 = f16[64,96,128]{2,1,0:T(8,128)(2,1)S(1)} all-to-all(f16[64,96,128]{2,1,0:T(8,128)(2,1)S(1)} %broadcast_in_dim.10), channel_id=1, replica_groups={{0,1,2,3,16,17,18,19,32,33,34,35,48,49,50,51,64,65,66,67,80,81,82,83,96..., dimensions={0} | all-to-all | bytes 3145728 | tf_op jit(solution)/shard_map/all_to_all | solution.py:510
  237.3 3.6 %collective-permute-start.30 = (f16[64,96,128]{2,1,0:T(8,128)(2,1)S(1)}, f16[64,96,128]{2,1,0:T(8,128)(2,1)S(1)}, u32[]{:S(2)}, u32[]{:S(2)}) collective-permute-start(f16[64,96,128]{2,1,0:T(8,128)(2,1)S(1)} %all_to_all.10), channel_id=1, source_target_pairs={{8,0},{0,8},{9,1},{1,9},{10,2},{2,10},{11,3},{3,11},{24,16},{16,24... | collective-permute-start | bytes 4718600 | tf_op jit(solution)/shard_map/ppermute | solution.py:38
  240.9 0.4 convert_element_type.34.here_ref
  241.3 2.6 %collective-permute-done.30 = f16[64,96,128]{2,1,0:T(8,128)(2,1)S(1)} collective-permute-done((f16[64,96,128]{2,1,0:T(8,128)(2,1)S(1)}, f16[64,96,128]{2,1,0:T(8,128)(2,1)S(1)}, u32[]{:S(2)}, u32[]{:S(2)}) %collective-permute-start.30) | collective-permute-done | bytes 1572896 | tf_op jit(solution)/shard_map/ppermute | solution.py:38
  244.0 0.4 convert_element_type.35.there_ref
  244.4 2.8 %shard_map.92 = (f32[1408,1024]{1,0:T(8,128)}, f32[8,128]{1,0:T(8,128)S(1)}) custom-call(s32[1]{0:T(128)} %bitcast.place_ref, f32[64,96,128]{2,1,0:T(8,128)S(1)} %convert_element_type.34.here_ref, f32[64,96,128]{2,1,0:T(8,128)S(1)} %convert_element_type.35.there_ref), custom_call_target="tpu_custom_call" | custom-call | flops 1048576 | bytes 9437184 | tf_op jit(solution)/shard_map/pallas_call | solution.py:477
  247.2 0.5 slice.47
  (101 shorter events, 0.9 us)
Async XLA Ops:
  0.6 12.1 %collective-permute-start.2 = (bf16[128,1408]{1,0:T(8,128)(2,1)}, bf16[128,1408]{1,0:T(8,128)(2,1)S(1)}, u32[]{:S(2)}, u32[]{:S(2)}) collective-permute-start(bf16[128,1408]{1,0:T(8,128)(2,1)} %refs_0_.3), channel_id=1, source_target_pairs={{1,0},{9,8},{2,1},{10,9},{3,2},{11,10},{0,3},{8,11},{17,16},{25,24... | collective-permute-start | bytes 1081352 | tf_op jit(solution)/shard_map/ppermute | solution.py:38
  5.3 15.7 %collective-permute-start.4 = (bf16[128,1408]{1,0:T(8,128)(2,1)}, bf16[128,1408]{1,0:T(8,128)(2,1)S(1)}, u32[]{:S(2)}, u32[]{:S(2)}) collective-permute-start(bf16[128,1408]{1,0:T(8,128)(2,1)} %refs_0_.3), channel_id=1, source_target_pairs={{64,0},{72,8},{65,1},{73,9},{66,2},{74,10},{67,3},{75,11},{80,16},... | collective-permute-start | bytes 1081352 | tf_op jit(solution)/shard_map/ppermute | solution.py:38
  6.5 17.8 %collective-permute-start.8 = (bf16[128,1408]{1,0:T(8,128)(2,1)}, bf16[128,1408]{1,0:T(8,128)(2,1)S(1)}, u32[]{:S(2)}, u32[]{:S(2)}) collective-permute-start(bf16[128,1408]{1,0:T(8,128)(2,1)} %refs_0_.3), channel_id=1, source_target_pairs={{3,0},{11,8},{0,1},{8,9},{1,2},{9,10},{2,3},{10,11},{19,16},{27,24... | collective-permute-start | bytes 1081352 | tf_op jit(solution)/shard_map/ppermute | solution.py:38
  12.7 16.9 %copy-start.21 = (bf16[128,1408]{1,0:T(8,128)(2,1)}, bf16[128,1408]{1,0:T(8,128)(2,1)S(1)}, u32[]{:S(2)}) copy-start(bf16[128,1408]{1,0:T(8,128)(2,1)S(1)} %collective-permute-done.2.refs_1_) | copy-start | bytes 1081348
  12.7 11.6 %collective-permute-start.6 = (bf16[128,1408]{1,0:T(8,128)(2,1)S(1)}, bf16[128,1408]{1,0:T(8,128)(2,1)S(1)}, u32[]{:S(2)}, u32[]{:S(2)}) collective-permute-start(bf16[128,1408]{1,0:T(8,128)(2,1)S(1)} %collective-permute-done.2.refs_1_), channel_id=1, source_target_pairs={{64,0},{72,8},{65,1},{73,9},{66,2},{74,10},{67,3},{75,11},{80,16},... | collective-permute-start | bytes 1081352 | tf_op jit(solution)/shard_map/ppermute | solution.py:38
  16.4 18.4 %copy-start.1 = (bf16[256,1024]{1,0:T(8,128)(2,1)S(1)}, bf16[256,1024]{1,0:T(8,128)(2,1)}, u32[]{:S(2)}) copy-start(bf16[256,1024]{1,0:T(8,128)(2,1)} %shard_map.86.refs_2_) | copy-start | bytes 1572868
  16.5 12.4 %collective-permute-start.1 = (bf16[256,1024]{1,0:T(8,128)(2,1)}, bf16[256,1024]{1,0:T(8,128)(2,1)S(1)}, u32[]{:S(2)}, u32[]{:S(2)}) collective-permute-start(bf16[256,1024]{1,0:T(8,128)(2,1)} %shard_map.86.refs_2_), channel_id=1, source_target_pairs={{16,0},{24,8},{17,1},{25,9},{18,2},{26,10},{19,3},{27,11},{32,16},... | collective-permute-start | bytes 1572872 | tf_op jit(solution)/shard_map/ppermute | solution.py:38
  19.2 15.6 %collective-permute-start = (bf16[256,1024]{1,0:T(8,128)(2,1)}, bf16[256,1024]{1,0:T(8,128)(2,1)S(1)}, u32[]{:S(2)}, u32[]{:S(2)}) collective-permute-start(bf16[256,1024]{1,0:T(8,128)(2,1)} %shard_map.86.refs_2_), channel_id=1, source_target_pairs={{68,0},{76,8},{69,1},{77,9},{70,2},{78,10},{71,3},{79,11},{84,16},... | collective-permute-start | bytes 1572872 | tf_op jit(solution)/shard_map/ppermute | solution.py:38
  21.0 8.6 %copy-start.22 = (bf16[128,1408]{1,0:T(8,128)(2,1)}, bf16[128,1408]{1,0:T(8,128)(2,1)S(1)}, u32[]{:S(2)}) copy-start(bf16[128,1408]{1,0:T(8,128)(2,1)S(1)} %collective-permute-done.4.refs_3_) | copy-start | bytes 1081348
  21.0 16.9 %collective-permute-start.3 = (bf16[128,1408]{1,0:T(8,128)(2,1)S(1)}, bf16[128,1408]{1,0:T(8,128)(2,1)S(1)}, u32[]{:S(2)}, u32[]{:S(2)}) collective-permute-start(bf16[128,1408]{1,0:T(8,128)(2,1)S(1)} %collective-permute-done.2.refs_1_), channel_id=1, source_target_pairs={{1,0},{9,8},{2,1},{10,9},{3,2},{11,10},{0,3},{8,11},{17,16},{25,24... | collective-permute-start | bytes 1081352 | tf_op jit(solution)/shard_map/ppermute | solution.py:38
  24.3 5.2 %copy-start.23 = (bf16[128,1408]{1,0:T(8,128)(2,1)}, bf16[128,1408]{1,0:T(8,128)(2,1)S(1)}, u32[]{:S(2)}) copy-start(bf16[128,1408]{1,0:T(8,128)(2,1)S(1)} %collective-permute-done.8.refs_2_) | copy-start | bytes 1081348
  24.3 13.6 %collective-permute-start.5 = (bf16[128,1408]{1,0:T(8,128)(2,1)S(1)}, bf16[128,1408]{1,0:T(8,128)(2,1)S(1)}, u32[]{:S(2)}, u32[]{:S(2)}) collective-permute-start(bf16[128,1408]{1,0:T(8,128)(2,1)S(1)} %collective-permute-done.4.refs_3_), channel_id=1, source_target_pairs={{3,0},{11,8},{0,1},{8,9},{1,2},{9,10},{2,3},{10,11},{19,16},{27,24... | collective-permute-start | bytes 1081352 | tf_op jit(solution)/shard_map/ppermute | solution.py:38
  24.3 30.0 %copy-start.17 = (bf16[128,1408]{1,0:T(8,128)(2,1)}, bf16[128,1408]{1,0:T(8,128)(2,1)S(1)}, u32[]{:S(2)}) copy-start(bf16[128,1408]{1,0:T(8,128)(2,1)S(1)} %collective-permute-done.6.refs_1_) | copy-start | bytes 1081348
  24.3 13.6 %collective-permute-start.7 = (bf16[128,1408]{1,0:T(8,128)(2,1)S(1)}, bf16[128,1408]{1,0:T(8,128)(2,1)S(1)}, u32[]{:S(2)}, u32[]{:S(2)}) collective-permute-start(bf16[128,1408]{1,0:T(8,128)(2,1)S(1)} %collective-permute-done.6.refs_1_), channel_id=1, source_target_pairs={{1,0},{9,8},{2,1},{10,9},{3,2},{11,10},{0,3},{8,11},{17,16},{25,24... | collective-permute-start | bytes 1081352 | tf_op jit(solution)/shard_map/ppermute | solution.py:38
  28.9 30.7 %copy-start.2 = (bf16[256,1024]{1,0:T(8,128)(2,1)}, bf16[256,1024]{1,0:T(8,128)(2,1)S(1)}, u32[]{:S(2)}) copy-start(bf16[256,1024]{1,0:T(8,128)(2,1)S(1)} %collective-permute-done.1.refs_4_) | copy-start | bytes 1572868
  28.9 13.0 %collective-permute-start.10 = (bf16[256,1024]{1,0:T(8,128)(2,1)}, bf16[256,1024]{1,0:T(8,128)(2,1)S(1)}, u32[]{:S(2)}, u32[]{:S(2)}) collective-permute-start(bf16[256,1024]{1,0:T(8,128)(2,1)} %shard_map.86.refs_2_), channel_id=1, source_target_pairs={{48,0},{56,8},{49,1},{57,9},{50,2},{58,10},{51,3},{59,11},{0,16},{... | collective-permute-start | bytes 1572872 | tf_op jit(solution)/shard_map/ppermute | solution.py:38
  34.8 24.8 %copy-start.3 = (bf16[256,1024]{1,0:T(8,128)(2,1)}, bf16[256,1024]{1,0:T(8,128)(2,1)S(1)}, u32[]{:S(2)}) copy-start(bf16[256,1024]{1,0:T(8,128)(2,1)S(1)} %collective-permute-done.refs_3_) | copy-start | bytes 1572868
  34.8 10.6 %collective-permute-start.11 = (bf16[256,1024]{1,0:T(8,128)(2,1)S(1)}, bf16[256,1024]{1,0:T(8,128)(2,1)S(1)}, u32[]{:S(2)}, u32[]{:S(2)}) collective-permute-start(bf16[256,1024]{1,0:T(8,128)(2,1)S(1)} %copy-done.1), channel_id=1, source_target_pairs={{8,0},{0,8},{9,1},{1,9},{10,2},{2,10},{11,3},{3,11},{24,16},{16,24... | collective-permute-start | bytes 1572872 | tf_op jit(solution)/shard_map/ppermute | solution.py:38
  37.9 0.9 copy-start.19
  37.9 16.4 %copy-start.18 = (bf16[128,1408]{1,0:T(8,128)(2,1)}, bf16[128,1408]{1,0:T(8,128)(2,1)S(1)}, u32[]{:S(2)}) copy-start(bf16[128,1408]{1,0:T(8,128)(2,1)S(1)} %collective-permute-done.3.refs_0_) | copy-start | bytes 1081348
  38.0 0.9 copy-start.20
  38.8 12.0 %collective-permute-start.9 = (bf16[256,1024]{1,0:T(8,128)(2,1)S(1)}, bf16[256,1024]{1,0:T(8,128)(2,1)S(1)}, u32[]{:S(2)}, u32[]{:S(2)}) collective-permute-start(bf16[256,1024]{1,0:T(8,128)(2,1)S(1)} %collective-permute-done.1.refs_4_), channel_id=1, source_target_pairs={{68,0},{76,8},{69,1},{77,9},{70,2},{78,10},{71,3},{79,11},{84,16},... | collective-permute-start | bytes 1572872 | tf_op jit(solution)/shard_map/ppermute | solution.py:38
  41.9 17.7 %copy-start.4 = (bf16[256,1024]{1,0:T(8,128)(2,1)}, bf16[256,1024]{1,0:T(8,128)(2,1)S(1)}, u32[]{:S(2)}) copy-start(bf16[256,1024]{1,0:T(8,128)(2,1)S(1)} %collective-permute-done.10.refs_5_) | copy-start | bytes 1572868
  41.9 17.8 %collective-permute-start.14 = (bf16[256,1024]{1,0:T(8,128)(2,1)S(1)}, bf16[256,1024]{1,0:T(8,128)(2,1)S(1)}, u32[]{:S(2)}, u32[]{:S(2)}) collective-permute-start(bf16[256,1024]{1,0:T(8,128)(2,1)S(1)} %collective-permute-done.10.refs_5_), channel_id=1, source_target_pairs={{8,0},{0,8},{9,1},{1,9},{10,2},{2,10},{11,3},{3,11},{24,16},{16,24... | collective-permute-start | bytes 1572872 | tf_op jit(solution)/shard_map/ppermute | solution.py:38
  45.3 17.7 %collective-permute-start.15 = (bf16[256,1024]{1,0:T(8,128)(2,1)S(1)}, bf16[256,1024]{1,0:T(8,128)(2,1)S(1)}, u32[]{:S(2)}, u32[]{:S(2)}) collective-permute-start(bf16[256,1024]{1,0:T(8,128)(2,1)S(1)} %collective-permute-done.refs_3_), channel_id=1, source_target_pairs={{48,0},{56,8},{49,1},{57,9},{50,2},{58,10},{51,3},{59,11},{0,16},{... | collective-permute-start | bytes 1572872 | tf_op jit(solution)/shard_map/ppermute | solution.py:38
  45.3 18.3 %collective-permute-start.12 = (bf16[256,1024]{1,0:T(8,128)(2,1)S(1)}, bf16[256,1024]{1,0:T(8,128)(2,1)S(1)}, u32[]{:S(2)}, u32[]{:S(2)}) collective-permute-start(bf16[256,1024]{1,0:T(8,128)(2,1)S(1)} %collective-permute-done.refs_3_), channel_id=1, source_target_pairs={{8,0},{0,8},{9,1},{1,9},{10,2},{2,10},{11,3},{3,11},{24,16},{16,24... | collective-permute-start | bytes 1572872 | tf_op jit(solution)/shard_map/ppermute | solution.py:38
  45.4 14.3 %copy-start.5 = (bf16[256,1024]{1,0:T(8,128)(2,1)}, bf16[256,1024]{1,0:T(8,128)(2,1)S(1)}, u32[]{:S(2)}) copy-start(bf16[256,1024]{1,0:T(8,128)(2,1)S(1)} %collective-permute-done.11.refs_6_) | copy-start | bytes 1572868
  45.4 18.3 %collective-permute-start.16 = (bf16[256,1024]{1,0:T(8,128)(2,1)S(1)}, bf16[256,1024]{1,0:T(8,128)(2,1)S(1)}, u32[]{:S(2)}, u32[]{:S(2)}) collective-permute-start(bf16[256,1024]{1,0:T(8,128)(2,1)S(1)} %collective-permute-done.1.refs_4_), channel_id=1, source_target_pairs={{16,0},{24,8},{17,1},{25,9},{18,2},{26,10},{19,3},{27,11},{32,16},... | collective-permute-start | bytes 1572872 | tf_op jit(solution)/shard_map/ppermute | solution.py:38
  50.9 12.1 %copy-start.6 = (bf16[256,1024]{1,0:T(8,128)(2,1)}, bf16[256,1024]{1,0:T(8,128)(2,1)S(1)}, u32[]{:S(2)}) copy-start(bf16[256,1024]{1,0:T(8,128)(2,1)S(1)} %collective-permute-done.9.refs_4_.refs_12_) | copy-start | bytes 1572868
  50.9 13.2 %collective-permute-start.13 = (bf16[256,1024]{1,0:T(8,128)(2,1)S(1)}, bf16[256,1024]{1,0:T(8,128)(2,1)S(1)}, u32[]{:S(2)}, u32[]{:S(2)}) collective-permute-start(bf16[256,1024]{1,0:T(8,128)(2,1)S(1)} %collective-permute-done.1.refs_4_), channel_id=1, source_target_pairs={{8,0},{0,8},{9,1},{1,9},{10,2},{2,10},{11,3},{3,11},{24,16},{16,24... | collective-permute-start | bytes 1572872 | tf_op jit(solution)/shard_map/ppermute | solution.py:38
  59.7 4.4 %copy-start.7 = (bf16[256,1024]{1,0:T(8,128)(2,1)}, bf16[256,1024]{1,0:T(8,128)(2,1)S(1)}, u32[]{:S(2)}) copy-start(bf16[256,1024]{1,0:T(8,128)(2,1)S(1)} %collective-permute-done.14.refs_9_) | copy-start | bytes 1572868
  59.7 17.5 %collective-permute-start.20 = (bf16[256,1024]{1,0:T(8,128)(2,1)S(1)}, bf16[256,1024]{1,0:T(8,128)(2,1)S(1)}, u32[]{:S(2)}, u32[]{:S(2)}) collective-permute-start(bf16[256,1024]{1,0:T(8,128)(2,1)S(1)} %collective-permute-done.9.refs_4_.refs_12_), channel_id=1, source_target_pairs={{16,0},{24,8},{17,1},{25,9},{18,2},{26,10},{19,3},{27,11},{32,16},... | collective-permute-start | bytes 1572872 | tf_op jit(solution)/shard_map/ppermute | solution.py:38
  63.0 14.2 %copy-start.8 = (bf16[256,1024]{1,0:T(8,128)(2,1)}, bf16[256,1024]{1,0:T(8,128)(2,1)S(1)}, u32[]{:S(2)}) copy-start(bf16[256,1024]{1,0:T(8,128)(2,1)S(1)} %collective-permute-done.15.refs_2_.refs_10_) | copy-start | bytes 1572868
  63.0 14.4 %collective-permute-start.19 = (bf16[256,1024]{1,0:T(8,128)(2,1)S(1)}, bf16[256,1024]{1,0:T(8,128)(2,1)S(1)}, u32[]{:S(2)}, u32[]{:S(2)}) collective-permute-start(bf16[256,1024]{1,0:T(8,128)(2,1)S(1)} %collective-permute-done.9.refs_4_.refs_12_), channel_id=1, source_target_pairs={{8,0},{0,8},{9,1},{1,9},{10,2},{2,10},{11,3},{3,11},{24,16},{16,24... | collective-permute-start | bytes 1572872 | tf_op jit(solution)/shard_map/ppermute | solution.py:38
  63.6 0.8 copy-start.9
  63.6 13.8 %collective-permute-start.17 = (bf16[256,1024]{1,0:T(8,128)(2,1)S(1)}, bf16[256,1024]{1,0:T(8,128)(2,1)S(1)}, u32[]{:S(2)}, u32[]{:S(2)}) collective-permute-start(bf16[256,1024]{1,0:T(8,128)(2,1)S(1)} %collective-permute-done.15.refs_2_.refs_10_), channel_id=1, source_target_pairs={{8,0},{0,8},{9,1},{1,9},{10,2},{2,10},{11,3},{3,11},{24,16},{16,24... | collective-permute-start | bytes 1572872 | tf_op jit(solution)/shard_map/ppermute | solution.py:38
  63.7 13.5 %copy-start.10 = (bf16[256,1024]{1,0:T(8,128)(2,1)}, bf16[256,1024]{1,0:T(8,128)(2,1)S(1)}, u32[]{:S(2)}) copy-start(bf16[256,1024]{1,0:T(8,128)(2,1)S(1)} %collective-permute-done.16.refs_3_.refs_11_) | copy-start | bytes 1572868
  63.7 13.7 %collective-permute-start.18 = (bf16[256,1024]{1,0:T(8,128)(2,1)S(1)}, bf16[256,1024]{1,0:T(8,128)(2,1)S(1)}, u32[]{:S(2)}, u32[]{:S(2)}) collective-permute-start(bf16[256,1024]{1,0:T(8,128)(2,1)S(1)} %collective-permute-done.16.refs_3_.refs_11_), channel_id=1, source_target_pairs={{8,0},{0,8},{9,1},{1,9},{10,2},{2,10},{11,3},{3,11},{24,16},{16,24... | collective-permute-start | bytes 1572872 | tf_op jit(solution)/shard_map/ppermute | solution.py:38
  64.4 0.8 copy-start.11
  77.2 2.0 copy-start.12
  77.2 2.0 collective-permute-start.21
  77.4 1.9 copy-start.14
  77.4 1.8 copy-start.15
  77.4 1.8 copy-start.13
  79.2 0.8 copy-start.16
  80.1 24.5 %copy-start = (bf16[1024,1408]{1,0:T(8,128)(2,1)S(1)}, bf16[1024,1408]{1,0:T(8,128)(2,1)}, u32[]{:S(2)}) copy-start(bf16[1024,1408]{1,0:T(8,128)(2,1)} %get-tuple-element.66) | copy-start | bytes 8650756
  92.8 2.8 %collective-permute-start.22 = (f32[2,1024]{1,0:T(2,128)}, f32[2,1024]{1,0:T(2,128)S(1)}, u32[]{:S(2)}, u32[]{:S(2)}) collective-permute-start(f32[2,1024]{1,0:T(2,128)} %get-tuple-element.58), channel_id=1, source_target_pairs={{64,0},{72,8},{65,1},{73,9},{66,2},{74,10},{67,3},{75,11},{80,16},... | collective-permute-start | bytes 24584 | tf_op jit(solution)/shard_map/ppermute | solution.py:38
  92.9 3.5 %collective-permute-start.23 = (f32[16,256]{1,0:T(8,128)}, f32[16,256]{1,0:T(8,128)S(1)}, u32[]{:S(2)}, u32[]{:S(2)}) collective-permute-start(f32[16,256]{1,0:T(8,128)} %get-tuple-element.59), channel_id=1, source_target_pairs={{8,0},{0,8},{9,1},{1,9},{10,2},{2,10},{11,3},{3,11},{24,16},{16,24... | collective-permute-start | bytes 49160 | tf_op jit(solution)/shard_map/ppermute | solution.py:38
  97.2 5.2 %collective-permute-start.24 = (f32[2,1024]{1,0:T(2,128)S(1)}, f32[2,1024]{1,0:T(2,128)S(1)}, u32[]{:S(2)}, u32[]{:S(2)}) collective-permute-start(f32[2,1024]{1,0:T(2,128)S(1)} %multiply_add_fusion.6), channel_id=1, source_target_pairs={{1,0},{9,8},{2,1},{10,9},{3,2},{11,10},{0,3},{8,11},{17,16},{25,24... | collective-permute-start | bytes 24584 | tf_op jit(solution)/shard_map/ppermute | solution.py:38
  100.6 3.8 %collective-permute-start.25 = (f32[16,256]{1,0:T(8,128)S(1)}, f32[16,256]{1,0:T(8,128)S(1)}, u32[]{:S(2)}, u32[]{:S(2)}) collective-permute-start(f32[16,256]{1,0:T(8,128)S(1)} %multiply_add_fusion.3), channel_id=1, source_target_pairs={{68,0},{76,8},{69,1},{77,9},{70,2},{78,10},{71,3},{79,11},{84,16},... | collective-permute-start | bytes 49160 | tf_op jit(solution)/shard_map/ppermute | solution.py:38
  104.4 4.5 %collective-permute-start.26 = (f32[2,1024]{1,0:T(2,128)S(1)}, f32[2,1024]{1,0:T(2,128)S(1)}, u32[]{:S(2)}, u32[]{:S(2)}) collective-permute-start(f32[2,1024]{1,0:T(2,128)S(1)} %multiply_add_fusion.5), channel_id=1, source_target_pairs={{2,0},{10,8},{3,1},{11,9},{0,2},{8,10},{1,3},{9,11},{18,16},{26,24... | collective-permute-start | bytes 24584 | tf_op jit(solution)/shard_map/ppermute | solution.py:38
  107.4 2.6 %collective-permute-start.27 = (f32[16,256]{1,0:T(8,128)S(1)}, f32[16,256]{1,0:T(8,128)S(1)}, u32[]{:S(2)}, u32[]{:S(2)}) collective-permute-start(f32[16,256]{1,0:T(8,128)S(1)} %multiply_add_fusion.2), channel_id=1, source_target_pairs={{16,0},{24,8},{17,1},{25,9},{18,2},{26,10},{19,3},{27,11},{32,16},... | collective-permute-start | bytes 49160 | tf_op jit(solution)/shard_map/ppermute | solution.py:38
  110.1 4.2 %collective-permute-start.28 = (f32[16,256]{1,0:T(8,128)S(1)}, f32[16,256]{1,0:T(8,128)S(1)}, u32[]{:S(2)}, u32[]{:S(2)}) collective-permute-start(f32[16,256]{1,0:T(8,128)S(1)} %multiply_add_fusion.1), channel_id=1, source_target_pairs={{32,0},{40,8},{33,1},{41,9},{34,2},{42,10},{35,3},{43,11},{48,16},... | collective-permute-start | bytes 49160 | tf_op jit(solution)/shard_map/ppermute | solution.py:38
  145.6 10.2 %collective-permute-start.29 = (f32[64,88,128]{2,1,0:T(8,128)}, f32[64,88,128]{2,1,0:T(8,128)S(1)}, u32[]{:S(2)}, u32[]{:S(2)}) collective-permute-start(f32[64,88,128]{2,1,0:T(8,128)} %get-tuple-element.68), channel_id=1, source_target_pairs={{8,0},{0,8},{9,1},{1,9},{10,2},{2,10},{11,3},{3,11},{24,16},{16,24... | collective-permute-start | bytes 8650760 | tf_op jit(solution)/shard_map/ppermute | solution.py:38
  159.5 46.1 %all-to-all-start = ((f32[64,88,128]{2,1,0:T(8,128)}), f32[64,88,128]{2,1,0:T(8,128)S(1)}, u32[]{:S(2)}, u32[]{:S(2)}) async-start(f32[64,88,128]{2,1,0:T(8,128)} %add.64), calls=%async_computation | async-start | bytes 5767168 | tf_op jit(solution)/shard_map/all_to_all | solution.py:510
  237.3 6.7 %collective-permute-start.30 = (f16[64,96,128]{2,1,0:T(8,128)(2,1)S(1)}, f16[64,96,128]{2,1,0:T(8,128)(2,1)S(1)}, u32[]{:S(2)}, u32[]{:S(2)}) collective-permute-start(f16[64,96,128]{2,1,0:T(8,128)(2,1)S(1)} %all_to_all.10), channel_id=1, source_target_pairs={{8,0},{0,8},{9,1},{1,9},{10,2},{2,10},{11,3},{3,11},{24,16},{16,24... | collective-permute-start | bytes 4718600 | tf_op jit(solution)/shard_map/ppermute | solution.py:38
